TPU v7x, 256 devices: a whole 4x4x8 slice. The times are simulated.
256 devices in a mesh: expert: 32 (over z_lo, y, x), mp: 8 (over z_hi, core).
Axes of the slice: x: 4, y: 4, z: 8 (z_hi: 4, z_lo: 2; z = z_hi * 2 + z_lo), core: 2. Of those that a mesh axis runs over, the one named last changes fastest.
Arguments:
- attention: bfloat16 [4096, 3584], P('expert', 'mp'), may hold values from -6 to 6
- out_weight: bfloat16 [3584, 7168], P('expert', 'mp'), may hold values from -0.09375 to 0.09375
- residual: bfloat16 [4096, 7168], P('expert', 'mp')
- norm_gain: float32 [7168], P('mp'), may hold values from 0.5 to 2
- expert_ids: int32 [4096, 2], P('expert'), may hold values from 0 to 15, as said below
- slot_index: int32 [4096, 2], P('expert'), may hold values from -1 to 19, as said below
- gate_prob: float32 [4096, 2], P('expert'), may hold values from 0.1 to 1
- w_gate: bfloat16 [32, 7168, 2048], P('expert', None, 'mp'), may hold values from -0.0625 to 0.0625
- w_up: bfloat16 [32, 7168, 2048], P('expert', None, 'mp'), may hold values from -0.0625 to 0.0625
- w_down: bfloat16 [32, 2048, 7168], P('expert', 'mp'), may hold values from -0.09375 to 0.09375
Outputs:
- layer_out: bfloat16 [4096, 7168], P('expert', 'mp')
Inputs may be any that keep to these rules, and one draw needn't show every extreme that they name: `expert_ids`: each token names two different experts; in every block of 128 tokens some expert is named by more than 20 choices. `slot_index`: within each block of 128 tokens, the choices naming one expert take its slots 0, 1, 2, ... in order of token and then choice; those beyond its 20 slots get -1. Every block fills all slots of some expert.
All inputs are finite; a program needn't handle non-finite values.
Results may differ from a plain program's by a relative error of at most 0.0085.
Values may be sent and summed in bfloat16 or wider, within the bound.
No kernel may reach another device: no remote copies, remote signals or barrier semaphores. Data moves between devices by JAX's collectives and lax.ppermute only.
A program may use at most 128 MiB of HBM per device.

v0:
```python
import functools

import jax
import jax.numpy as jnp
from jax import lax
from jax.experimental import pallas as pl
from jax.experimental.pallas import tpu as pltpu
from jax.sharding import Mesh
from jax.sharding import PartitionSpec as P

epsilon = 1e-05

EXPERT = ("z_lo", "y", "x")
MP = ("z_hi", "core")
SIZES = (2, 4, 4, 4, 2)
NX = 4
NY = 4
NZ = 4
N_MP = 8

TOK = 128
D = 7168
SHARD = D // N_MP
FEAT = 448
W_ROWS = 112
GROUPS = 32
HID = 256
SHARE = 10
CHUNK = 5
UNITS = 5
QUARTER = D // NZ
ROWS = GROUPS * 8
FOUR = GROUPS * 4
SLOTS = GROUPS * CHUNK
GAIN_ROWS = 8

BF16 = jnp.bfloat16
F32 = jnp.float32
MIB = 1024 * 1024


def dot(a, b, dims=((1,), (0,))):
    return lax.dot_general(a, b, (dims, ((), ())), preferred_element_type=F32)


def iota(shape, dim):
    return lax.broadcasted_iota(jnp.int32, shape, dim)


def shift(value, axis, size, step):
    if step == 0:
        return value
    return lax.ppermute(value, axis, [(i, (i + step) % size) for i in range(size)])


def swap(value, axis):
    return lax.ppermute(value, axis, [(0, 1), (1, 0)])


def shard_of(place, step, other):
    z = lax.rem(place[0] - step + NZ, NZ)
    core = 1 - place[1] if other else place[1]
    return 2 * z + core


def call(kernel, out_shape, flops, moved, limit=24, **kwargs):
    return pl.pallas_call(
        kernel,
        out_shape=out_shape,
        compiler_params=pltpu.CompilerParams(vmem_limit_bytes=limit * MIB),
        cost_estimate=pl.CostEstimate(flops=flops, bytes_accessed=moved, transcendentals=0),
        **kwargs,
    )


SMEM = pl.BlockSpec(memory_space=pltpu.SMEM)


def whole(shape):
    return pl.BlockSpec(shape, lambda step: (0,) * len(shape))


def project_kernel(place, *refs):
    features, blocks, outs = refs[:8], refs[8:12], refs[12:16]
    rows, weights = refs[16:]
    for other in range(2):
        for step in range(NZ):
            rows[shard_of(place, step, other)] = features[other * NZ + step][...]
    for step in range(NX):
        x = lax.rem(place[3] - step + NX, NX)
        weights[place[2] * NX + x] = blocks[step][0:W_ROWS]
        weights[(1 - place[2]) * NX + x] = blocks[step][W_ROWS:]
    near = weights[0:NX].reshape(FEAT, SHARD)
    later = weights[NX:].reshape(FEAT, SHARD)
    for step, out in enumerate(outs):
        y = lax.rem(place[4] + step, NY)
        total = dot(rows[y], near, ((0,), (0,))) + dot(rows[NY + y], later, ((0,), (0,)))
        out[...] = total.astype(out.dtype)


def project(place, attention, out_weight, residual):
    flipped = attention.T
    features = []
    for step in range(NZ):
        pairs = []
        for y in range(NY):
            for m in range(N_MP):
                z, core = divmod(m // NY * NY + y, 2)
                pairs.append((y * N_MP + m, m % NY * N_MP + (z + step) % NZ * 2 + core))
        features.append(lax.ppermute(flipped, ("y",) + MP, pairs))
    features += [swap(value, "core") for value in features]
    both = jnp.concatenate([out_weight, swap(out_weight, "z_lo")], axis=0)
    blocks = [shift(both, "x", NX, step) for step in range(NX)]
    partial = call(
        project_kernel,
        [jax.ShapeDtypeStruct((TOK, SHARD), BF16 if step else F32) for step in range(NY)],
        2 * NY * TOK * 2 * FEAT * SHARD,
        4_000_000,
        16,
        grid=(1,),
        in_specs=[SMEM] + [whole((FEAT, TOK))] * 8 + [whole((2 * W_ROWS, SHARD))] * 4,
        out_specs=[whole((TOK, SHARD))] * NY,
        scratch_shapes=[
            pltpu.VMEM((N_MP, FEAT, TOK), BF16),
            pltpu.VMEM((2 * NX, W_ROWS, SHARD), BF16),
        ],
    )(place, *features, *blocks)
    total = residual.astype(F32) + partial[0]
    for step in range(1, NY):
        total = total + shift(partial[step], "y", NY, step).astype(F32)
    return total


def unit_rows(index, single):
    group = lax.shift_right_logical(index, 3)
    if single:
        return (index & 7) * GROUPS + group
    return (lax.shift_right_logical(index, 2) & 1) * FOUR + group * 4 + (index & 3)


def selection(single, back):
    shape = (ROWS, ROWS)
    hit = iota(shape, int(back)) == unit_rows(iota(shape, 1 - int(back)), single)
    return hit.astype(F32).astype(BF16)


def columns(j):
    return slice(j % 2 * SHARD, (j % 2 + 1) * SHARD)


def by_features(units, rows):
    pick = selection(False, False)
    for unit in range(4):
        value = dot(pick, units[:, unit].reshape(ROWS, SHARD)).astype(BF16)
        for half in range(2):
            j = 4 * half + unit
            rows[j // 2, 0:FOUR, columns(j)] = value[half * FOUR : (half + 1) * FOUR]
    value = dot(selection(True, False), units[:, 4].reshape(ROWS, SHARD)).astype(BF16)
    for j in range(N_MP):
        rows[j // 2, FOUR:, columns(j)] = value[j * GROUPS : (j + 1) * GROUPS]


def by_units(rows, out):
    pick = selection(False, True)
    for unit in range(4):
        halves = [rows[j // 2, 0:FOUR, columns(j)] for j in (unit, 4 + unit)]
        value = dot(pick, jnp.concatenate(halves, axis=0)).astype(BF16)
        out[:, unit] = value.reshape(GROUPS, 8, SHARD)
    eighths = [rows[j // 2, FOUR:, columns(j)] for j in range(N_MP)]
    value = dot(selection(True, True), jnp.concatenate(eighths, axis=0)).astype(BF16)
    out[:, 4] = value.reshape(GROUPS, 8, SHARD)


def slot_codes(shape, dim, chunk):
    index = iota(shape, dim)
    four = lax.shift_right_logical(index, 3) * 16 + (index & 3)
    fifth = lax.shift_right_logical(index - FOUR, 1) * 16 + 4
    return jnp.where(index < FOUR, four, fifth) + chunk * CHUNK


def send_rows(codes, chunk, normed, out, rows):
    slots = slot_codes((SLOTS, TOK), 0, chunk)
    hit = (slots == codes[0:1, :]) | (slots == codes[1:2, :])
    assign = hit.astype(F32).astype(BF16)
    for j in range(N_MP):
        rows[j // 2, :, columns(j)] = dot(assign, normed[j]).astype(BF16)
    by_units(rows, out)


def first_kernel(place, codes, *refs):
    parts, normed, out, rows = refs[:8], refs[8], refs[9], refs[10]
    total = jnp.zeros((TOK, 1), F32)
    for part in parts:
        value = part[...].astype(F32)[0:TOK]
        total = total + jnp.sum(value * value, axis=1, keepdims=True)
    scale = lax.rsqrt(total / D + epsilon)
    for other in range(2):
        for step in range(NZ):
            lines = parts[other * NZ + step][...].astype(F32)
            gain = lines[TOK : TOK + 1] + lines[TOK + 1 : TOK + 2] + lines[TOK + 2 : TOK + 3]
            value = lines[0:TOK] * scale * gain
            normed[shard_of(place, step, other)] = value.astype(BF16)
    send_rows(codes, 0, normed, out, rows)


def second_kernel(codes, normed, out, rows):
    send_rows(codes, 1, normed, out, rows)


SLAB = (GROUPS, UNITS, 8, SHARD)
SLAB_SHAPE = pltpu.HBM(SLAB, BF16)
ROW_SCRATCH = pltpu.VMEM((NZ, SLOTS, QUARTER), BF16)


def dispatch(place, codes, hidden_state, norm_gain):
    lines = jnp.zeros((GAIN_ROWS, SHARD), F32).at[0:3].set(jnp.stack(terms_of(norm_gain)))
    mine = jnp.concatenate([hidden_state, lines], axis=0).astype(BF16)
    parts = [shift(mine, "z_hi", NZ, step) for step in range(NZ)]
    parts += [swap(value, "core") for value in parts]
    normed, one = call(
        first_kernel,
        (pltpu.HBM((N_MP, TOK, SHARD), BF16), SLAB_SHAPE),
        2_000_000_000,
        6_000_000,
        grid=(1,),
        in_specs=[SMEM, whole((2, TOK))] + [whole((TOK + GAIN_ROWS, SHARD))] * 8,
        out_specs=[whole((N_MP, TOK, SHARD)), whole(SLAB)],
        scratch_shapes=[ROW_SCRATCH],
    )(place, codes, *parts)
    two = call(
        second_kernel,
        SLAB_SHAPE,
        1_000_000_000,
        4_000_000,
        grid=(1,),
        in_specs=[whole((2, TOK)), whole((N_MP, TOK, SHARD))],
        out_specs=whole(SLAB),
        scratch_shapes=[ROW_SCRATCH],
    )(codes, normed)
    return one, two


def terms_of(value):
    first = lax.reduce_precision(value, 8, 7)
    second = lax.reduce_precision(value - first, 8, 7)
    return [first, second, value - first - second]


def experts_kernel(units, gate_a, up_a, gate_b, up_b, down_a, down_b, out, rows, sums, active):
    step = pl.program_id(0)

    @pl.when(step == 0)
    def _():
        by_features(units, rows)
        sums[...] = jnp.zeros_like(sums)

    @pl.when(step < NZ)
    def _():
        for index, weight in enumerate((gate_a, up_a, gate_b, up_b)):
            sums[index] = sums[index] + dot(rows[step], weight[...])

    @pl.when(step == NZ)
    def _():
        for index in range(2):
            active[index] = (jax.nn.silu(sums[2 * index]) * sums[2 * index + 1]).astype(BF16)

    @pl.when(step >= NZ)
    def _():
        rows[step - NZ] = (dot(active[0], down_a[...]) + dot(active[1], down_b[...])).astype(BF16)

    @pl.when(step == 2 * NZ - 1)
    def _():
        by_units(rows, out)


def experts(arrived, gate, up, down):
    first = lambda step: (jnp.minimum(step, NZ - 1), 0)
    second = lambda step: (0, jnp.maximum(step - NZ, 0))
    return call(
        experts_kernel,
        SLAB_SHAPE,
        2 * SLOTS * D * HID * 6,
        27_000_000,
        34,
        grid=(2 * NZ,),
        in_specs=[whole(SLAB)]
        + [pl.BlockSpec((QUARTER, HID), first)] * 4
        + [pl.BlockSpec((HID, QUARTER), second)] * 2,
        out_specs=whole(SLAB),
        scratch_shapes=[
            ROW_SCRATCH,
            pltpu.VMEM((4, SLOTS, HID), F32),
            pltpu.VMEM((2, SLOTS, HID), BF16),
        ],
    )(arrived, gate[0], up[0], gate[1], up[1], down[0], down[1])


def combine_kernel(chunk, place, codes, probs, units, keep, give, rows, weights):
    step = pl.program_id(0)

    @pl.when(step == 0)
    def _():
        by_features(units, rows)
        slots = slot_codes((TOK, SLOTS), 1, chunk)
        mixed = jnp.zeros((TOK, SLOTS), F32)
        for choice in range(2):
            hit = slots == codes[:, choice : choice + 1]
            mixed = mixed + jnp.where(hit, probs[:, choice : choice + 1], 0.0)
        upper = mixed.astype(BF16)
        weights[0] = upper
        weights[1] = (mixed - upper.astype(F32)).astype(BF16)

    value = rows[step]
    value = (dot(weights[0], value) + dot(weights[1], value)).astype(BF16)

    @pl.when(place[1] == 0)
    def _():
        keep[0], give[0] = value[:, :SHARD], value[:, SHARD:]

    @pl.when(place[1] == 1)
    def _():
        keep[0], give[0] = value[:, SHARD:], value[:, :SHARD]


def combine_chunk(chunk, place, codes, probs, returned):
    shape = jax.ShapeDtypeStruct((NZ, TOK, SHARD), BF16)
    keep, give = call(
        functools.partial(combine_kernel, chunk),
        (shape, shape),
        2_500_000_000,
        6_000_000,
        grid=(NZ,),
        in_specs=[SMEM, whole((TOK, 2)), whole((TOK, 2)), whole(SLAB)],
        out_specs=[pl.BlockSpec((1, TOK, SHARD), lambda step: (step, 0, 0))] * 2,
        scratch_shapes=[ROW_SCRATCH, pltpu.VMEM((2, TOK, SLOTS), BF16)],
    )(place, codes, probs, returned)
    return keep.astype(F32) + swap(give, "core").astype(F32)


def combine(place, codes, probs, returned):
    early = lax.optimization_barrier(combine_chunk(0, place, codes, probs, returned[0]).astype(BF16))
    both = (combine_chunk(1, place, codes, probs, returned[1]) + early.astype(F32)).astype(BF16)
    total = lax.dynamic_index_in_dim(both, place[0], 0, False).astype(F32)
    for step in range(1, NZ):
        piece = lax.dynamic_index_in_dim(both, lax.rem(place[0] + step, NZ), 0, False)
        total = total + shift(piece, "z_hi", NZ, step).astype(F32)
    return total


def shards(
    attention,
    out_weight,
    residual,
    norm_gain,
    expert_ids,
    slot_index,
    gate_prob,
    w_gate,
    w_up,
    w_down,
):
    place = jnp.stack([lax.axis_index(name) for name in ("z_hi", "core", "z_lo", "x", "y")])
    place = place.astype(jnp.int32)
    slot = slot_index - SHARE * place[1]
    codes = jnp.where((slot_index >= 0) & (slot >= 0) & (slot < SHARE), 16 * expert_ids + slot, -1)

    hidden_state = project(place, attention, out_weight, residual)
    one, two = dispatch(place, codes.T, hidden_state, norm_gain)
    one, gate, up, down = lax.optimization_barrier((one, w_gate[0], w_up[0], w_down[0]))
    gate, up, down = [(value, swap(value, "core")) for value in (gate, up, down)]
    two, gate, up, down = lax.optimization_barrier((two, gate, up, down))
    returned = []
    for rows in (one, two):
        arrived = lax.all_to_all(rows, EXPERT, split_axis=0, concat_axis=0, tiled=True)
        half_out = experts(arrived, gate, up, down)
        returned.append(lax.all_to_all(half_out, EXPERT, split_axis=0, concat_axis=0, tiled=True))
    expert_mix = combine(place, codes, gate_prob, returned)
    return (hidden_state + expert_mix).astype(BF16)


def solution(mesh):
    fine = Mesh(mesh.devices.reshape(SIZES), EXPERT + MP)
    return jax.shard_map(
        shards,
        mesh=fine,
        in_specs=(
            P(EXPERT, MP),
            P(EXPERT, MP),
            P(EXPERT, MP),
            P(MP),
            P(EXPERT, None),
            P(EXPERT, None),
            P(EXPERT, None),
            P(EXPERT, None, MP),
            P(EXPERT, None, MP),
            P(EXPERT, MP, None),
        ),
        out_specs=P(EXPERT, MP),
        check_vma=False,
    )
```

profile of v0, /device:TPU:1, one launch (start us, length us, event | category | flops | bytes accessed | tf_op | source)
XLA Modules:
  0.0 272.7 jit_solution(4104302585033882248)
XLA Ops:
  0.0 2.5 collective-permute-start.8
  2.5 4.0 %collective-permute-start = (bf16[448,128]{1,0:T(8,128)(2,1)}, bf16[448,128]{1,0:T(8,128)(2,1)S(1)}, u32[]{:S(2)}, u32[]{:S(2)}) collective-permute-start(bf16[448,128]{1,0:T(8,128)(2,1)} %bitcast.29), channel_id=1, source_target_pairs={{0,0},{1,32},{2,64},{3,96},{4,4},{5,36},{6,68},{7,100},{32,1},{33,... | collective-permute-start | bytes 344072 | tf_op jit(solution)/shard_map/ppermute | solution.py:110
  6.5 2.8 %collective-permute-start.1 = (bf16[448,128]{1,0:T(8,128)(2,1)}, bf16[448,128]{1,0:T(8,128)(2,1)S(1)}, u32[]{:S(2)}, u32[]{:S(2)}) collective-permute-start(bf16[448,128]{1,0:T(8,128)(2,1)} %bitcast.30), channel_id=1, source_target_pairs={{0,2},{1,34},{2,66},{3,98},{4,6},{5,38},{6,70},{7,102},{32,3},{33,... | collective-permute-start | bytes 344072 | tf_op jit(solution)/shard_map/ppermute | solution.py:110
  10.3 2.8 %collective-permute-start.10 = (bf16[224,896]{1,0:T(8,128)(2,1)S(1)}, bf16[224,896]{1,0:T(8,128)(2,1)S(1)}, u32[]{:S(2)}, u32[]{:S(2)}) collective-permute-start(bf16[224,896]{1,0:T(8,128)(2,1)S(1)} %constant_dynamic-update-slice_fusion.refs_8_), channel_id=1, source_target_pairs={{0,16},{8,24},{16,0},{24,8},{1,17},{9,25},{17,1},{25,9},{2,18},{10... | collective-permute-start | bytes 1204232 | tf_op jit(solution)/shard_map/ppermute | solution.py:53
  14.6 8.8 %collective-permute-start.2 = (bf16[448,128]{1,0:T(8,128)(2,1)}, bf16[448,128]{1,0:T(8,128)(2,1)S(1)}, u32[]{:S(2)}, u32[]{:S(2)}) collective-permute-start(bf16[448,128]{1,0:T(8,128)(2,1)} %bitcast.31), channel_id=1, source_target_pairs={{0,4},{1,36},{2,68},{3,100},{4,0},{5,32},{6,64},{7,96},{32,5},{33,... | collective-permute-start | bytes 344072 | tf_op jit(solution)/shard_map/ppermute | solution.py:110
  23.4 5.1 %collective-permute-done.2.refs_2_ = bf16[448,128]{1,0:T(8,128)(2,1)S(1)} collective-permute-done((bf16[448,128]{1,0:T(8,128)(2,1)}, bf16[448,128]{1,0:T(8,128)(2,1)S(1)}, u32[]{:S(2)}, u32[]{:S(2)}) %collective-permute-start.2) | collective-permute-done | bytes 114720 | tf_op jit(solution)/shard_map/ppermute | solution.py:110
  28.5 5.1 %collective-permute-done.3.refs_3_ = bf16[448,128]{1,0:T(8,128)(2,1)S(1)} collective-permute-done((bf16[448,128]{1,0:T(8,128)(2,1)}, bf16[448,128]{1,0:T(8,128)(2,1)S(1)}, u32[]{:S(2)}, u32[]{:S(2)}) %collective-permute-start.3) | collective-permute-done | bytes 114720 | tf_op jit(solution)/shard_map/ppermute | solution.py:110
  36.8 2.0 shard_map.100
  38.9 2.2 collective-permute-start.13
  42.3 5.1 %collective-permute-done.12 = bf16[128,896]{1,0:T(8,128)(2,1)S(1)} collective-permute-done((bf16[128,896]{1,0:T(8,128)(2,1)S(1)}, bf16[128,896]{1,0:T(8,128)(2,1)S(1)}, u32[]{:S(2)}, u32[]{:S(2)}) %collective-permute-start.12) | collective-permute-done | bytes 229408 | tf_op jit(solution)/shard_map/ppermute | solution.py:53
  47.4 4.1 %collective-permute-done.13 = bf16[128,896]{1,0:T(8,128)(2,1)S(1)} collective-permute-done((bf16[128,896]{1,0:T(8,128)(2,1)S(1)}, bf16[128,896]{1,0:T(8,128)(2,1)S(1)}, u32[]{:S(2)}, u32[]{:S(2)}) %collective-permute-start.13) | collective-permute-done | bytes 229408 | tf_op jit(solution)/shard_map/ppermute | solution.py:53
  52.5 6.3 %collective-permute-start.16 = (bf16[136,896]{1,0:T(8,128)(2,1)S(1)}, bf16[136,896]{1,0:T(8,128)(2,1)S(1)}, u32[]{:S(2)}, u32[]{:S(2)}) collective-permute-start(bf16[136,896]{1,0:T(8,128)(2,1)S(1)} %pad_maximum_fusion.refs_0_), channel_id=1, source_target_pairs={{0,4},{2,6},{4,0},{6,2},{1,5},{3,7},{5,1},{7,3},{8,12},{10,14},{12... | collective-permute-start | bytes 731144 | tf_op jit(solution)/shard_map/ppermute | solution.py:53
  58.8 2.2 collective-permute-start.18
  60.9 7.6 %collective-permute-done.15.refs_1_ = bf16[136,896]{1,0:T(8,128)(2,1)S(1)} collective-permute-done((bf16[136,896]{1,0:T(8,128)(2,1)S(1)}, bf16[136,896]{1,0:T(8,128)(2,1)S(1)}, u32[]{:S(2)}, u32[]{:S(2)}) %collective-permute-start.15) | collective-permute-done | bytes 243744 | tf_op jit(solution)/shard_map/ppermute | solution.py:53
  69.3 3.6 %collective-permute-done.16.refs_2_ = bf16[136,896]{1,0:T(8,128)(2,1)S(1)} collective-permute-done((bf16[136,896]{1,0:T(8,128)(2,1)S(1)}, bf16[136,896]{1,0:T(8,128)(2,1)S(1)}, u32[]{:S(2)}, u32[]{:S(2)}) %collective-permute-start.16) | collective-permute-done | bytes 243744 | tf_op jit(solution)/shard_map/ppermute | solution.py:53
  72.9 8.4 %collective-permute-start.20 = (bf16[136,896]{1,0:T(8,128)(2,1)S(1)}, bf16[136,896]{1,0:T(8,128)(2,1)S(1)}, u32[]{:S(2)}, u32[]{:S(2)}) collective-permute-start(bf16[136,896]{1,0:T(8,128)(2,1)S(1)} %collective-permute-done.16.refs_2_), channel_id=1, source_target_pairs={{0,1},{1,0},{2,3},{3,2},{4,5},{5,4},{6,7},{7,6},{8,9},{9,8},{10,11... | collective-permute-start | bytes 731144 | tf_op jit(solution)/shard_map/ppermute | solution.py:57
  83.8 4.5 %shard_map.101 = (bf16[8,128,896]{2,1,0:T(8,128)(2,1)}, bf16[32,5,8,896]{3,2,1,0:T(8,128)(2,1)}) custom-call(s32[5]{0:T(128)S(1)} %stack.39.place, s32[2,128]{1,0:T(2,128)S(1)} %copy.31.codes, bf16[136,896]{1,0:T(8,128)(2,1)S(1)} %pad_maximum_fusion.refs_0_, bf16[136,896]{1,0:T(8,128)(2,1)S(1)} %collective-permute-done.15.refs_1_, ...), custom_call_target="tpu_custom_call" | custom-call | flops 2000000000 | bytes 6000000 | tf_op jit(solution)/shard_map/pallas_call | solution.py:220
  88.4 5.8 %all-to-all-start.2 = ((bf16[32,5,8,896]{3,2,1,0:T(8,128)(2,1)}), bf16[32,5,8,896]{3,2,1,0:T(8,128)(2,1)S(1)}, u32[]{:S(2)}, u32[]{:S(2)}) async-start(bf16[32,5,8,896]{3,2,1,0:T(8,128)(2,1)} %get-tuple-element.56), calls=%async_computation.2 | async-start | bytes 4587520 | tf_op jit(solution)/shard_map/all_to_all | solution.py:374
  96.9 2.9 %shard_map.102 = bf16[32,5,8,896]{3,2,1,0:T(8,128)(2,1)} custom-call(s32[2,128]{1,0:T(2,128)S(1)} %copy.31.codes, bf16[8,128,896]{2,1,0:T(8,128)(2,1)S(1)} %copy-done.12), custom_call_target="tpu_custom_call" | custom-call | flops 1000000000 | bytes 4000000 | tf_op jit(solution)/shard_map/pallas_call | solution.py:230
  103.1 8.6 %collective-permute-done.23.up_b = bf16[7168,256]{1,0:T(8,128)(2,1)S(1)} collective-permute-done((bf16[7168,256]{1,0:T(8,128)(2,1)}, bf16[7168,256]{1,0:T(8,128)(2,1)S(1)}, u32[]{:S(2)}, u32[]{:S(2)}) %collective-permute-start.23) | collective-permute-done | bytes 3670048 | tf_op jit(solution)/shard_map/ppermute | solution.py:57
  113.5 9.5 %all-to-all-done.2.units = bf16[32,5,8,896]{3,2,1,0:T(8,128)(2,1)S(1)} async-done(((bf16[32,5,8,896]{3,2,1,0:T(8,128)(2,1)}), bf16[32,5,8,896]{3,2,1,0:T(8,128)(2,1)S(1)}, u32[]{:S(2)}, u32[]{:S(2)}) %all-to-all-start.2) | async-done | bytes 2293792 | tf_op jit(solution)/shard_map/all_to_all | solution.py:374
  123.0 7.2 %all-to-all-start = ((bf16[32,5,8,896]{3,2,1,0:T(8,128)(2,1)}), bf16[32,5,8,896]{3,2,1,0:T(8,128)(2,1)}, u32[]{:S(2)}, u32[]{:S(2)}) async-start(bf16[32,5,8,896]{3,2,1,0:T(8,128)(2,1)} %shard_map.102), calls=%async_computation | async-start | bytes 4587520 | tf_op jit(solution)/shard_map/all_to_all | solution.py:374
  130.2 2.0 copy-done
  132.2 2.0 copy-done.2
  134.3 2.0 copy-done.4
  136.3 2.0 copy-done.7
  138.3 2.0 copy-done.10
  140.4 11.0 %shard_map.105 = bf16[32,5,8,896]{3,2,1,0:T(8,128)(2,1)} custom-call(bf16[32,5,8,896]{3,2,1,0:T(8,128)(2,1)S(1)} %all-to-all-done.2.units, bf16[7168,256]{1,0:T(8,128)(2,1)S(1)} %bitcast.20, bf16[7168,256]{1,0:T(8,128)(2,1)S(1)} %bitcast.23, bf16[7168,256]{1,0:T(8,128)(2,1)S(1)} %copy-done.7, bf16[7168,256]{1,0:T(8,128)(2,1)S(1)} %copy-done.10, ...), custom_call_target="tpu_custom_call" | custom-call | flops 3523215360 | bytes 27000000 | tf_op jit(solution)/shard_map/pallas_call | solution.py:279
  151.4 7.0 %all-to-all-done.units = bf16[32,5,8,896]{3,2,1,0:T(8,128)(2,1)} async-done(((bf16[32,5,8,896]{3,2,1,0:T(8,128)(2,1)}), bf16[32,5,8,896]{3,2,1,0:T(8,128)(2,1)}, u32[]{:S(2)}, u32[]{:S(2)}) %all-to-all-start) | async-done | bytes 2293792 | tf_op jit(solution)/shard_map/all_to_all | solution.py:374
  158.4 7.4 %all-to-all-start.3 = ((bf16[32,5,8,896]{3,2,1,0:T(8,128)(2,1)}), bf16[32,5,8,896]{3,2,1,0:T(8,128)(2,1)S(1)}, u32[]{:S(2)}, u32[]{:S(2)}) async-start(bf16[32,5,8,896]{3,2,1,0:T(8,128)(2,1)} %shard_map.105), calls=%async_computation.3 | async-start | bytes 4587520 | tf_op jit(solution)/shard_map/all_to_all | solution.py:376
  165.8 2.0 copy-done.1
  167.9 2.0 copy-done.3
  169.9 2.0 copy-done.5
  171.9 2.0 copy-done.8
  174.0 2.0 copy-done.11
  176.0 11.8 %shard_map.103 = bf16[32,5,8,896]{3,2,1,0:T(8,128)(2,1)} custom-call(bf16[32,5,8,896]{3,2,1,0:T(8,128)(2,1)} %all-to-all-done.units, bf16[7168,256]{1,0:T(8,128)(2,1)S(1)} %bitcast.21, bf16[7168,256]{1,0:T(8,128)(2,1)S(1)} %bitcast.24, bf16[7168,256]{1,0:T(8,128)(2,1)S(1)} %copy-done.8, bf16[7168,256]{1,0:T(8,128)(2,1)S(1)} %copy-done.11, ...), custom_call_target="tpu_custom_call" | custom-call | flops 3523215360 | bytes 27000000 | tf_op jit(solution)/shard_map/pallas_call | solution.py:279
  187.9 6.6 %all-to-all-done.3.units = bf16[32,5,8,896]{3,2,1,0:T(8,128)(2,1)S(1)} async-done(((bf16[32,5,8,896]{3,2,1,0:T(8,128)(2,1)}), bf16[32,5,8,896]{3,2,1,0:T(8,128)(2,1)S(1)}, u32[]{:S(2)}, u32[]{:S(2)}) %all-to-all-start.3) | async-done | bytes 2293792 | tf_op jit(solution)/shard_map/all_to_all | solution.py:376
  194.5 7.3 %all-to-all-start.1 = ((bf16[32,5,8,896]{3,2,1,0:T(8,128)(2,1)}), bf16[32,5,8,896]{3,2,1,0:T(8,128)(2,1)}, u32[]{:S(2)}, u32[]{:S(2)}) async-start(bf16[32,5,8,896]{3,2,1,0:T(8,128)(2,1)} %shard_map.103), calls=%async_computation.1 | async-start | bytes 4587520 | tf_op jit(solution)/shard_map/all_to_all | solution.py:376
  201.9 4.2 %shard_map.106 = (bf16[4,128,896]{2,1,0:T(8,128)(2,1)S(1)}, bf16[4,128,896]{2,1,0:T(8,128)(2,1)}) custom-call(s32[5]{0:T(128)S(1)} %stack.39.place, s32[128,2]{1,0:T(8,128)S(1)} %add_select_fusion.codes, f32[128,2]{1,0:T(8,128)S(1)} %copy.32.probs, bf16[32,5,8,896]{3,2,1,0:T(8,128)(2,1)S(1)} %all-to-all-done.3.units), custom_call_target="tpu_custom_call" | custom-call | flops 2500000000 | bytes 6000000 | tf_op jit(solution)/shard_map/pallas_call | solution.py:327
  208.2 22.2 %all-to-all-done.1.units = bf16[32,5,8,896]{3,2,1,0:T(8,128)(2,1)} async-done(((bf16[32,5,8,896]{3,2,1,0:T(8,128)(2,1)}), bf16[32,5,8,896]{3,2,1,0:T(8,128)(2,1)}, u32[]{:S(2)}, u32[]{:S(2)}) %all-to-all-start.1) | async-done | bytes 2293792 | tf_op jit(solution)/shard_map/all_to_all | solution.py:376
  230.4 5.3 %shard_map.104 = (bf16[4,128,896]{2,1,0:T(8,128)(2,1)S(1)}, bf16[4,128,896]{2,1,0:T(8,128)(2,1)}) custom-call(s32[5]{0:T(128)S(1)} %stack.39.place, s32[128,2]{1,0:T(8,128)S(1)} %add_select_fusion.codes, f32[128,2]{1,0:T(8,128)S(1)} %copy.32.probs, bf16[32,5,8,896]{3,2,1,0:T(8,128)(2,1)} %all-to-all-done.1.units), custom_call_target="tpu_custom_call" | custom-call | flops 2500000000 | bytes 6000000 | tf_op jit(solution)/shard_map/pallas_call | solution.py:327
  235.7 3.5 %collective-permute-start.25 = (bf16[4,128,896]{2,1,0:T(8,128)(2,1)}, bf16[4,128,896]{2,1,0:T(8,128)(2,1)}, u32[]{:S(2)}, u32[]{:S(2)}) collective-permute-start(bf16[4,128,896]{2,1,0:T(8,128)(2,1)} %get-tuple-element.55), channel_id=1, source_target_pairs={{0,1},{1,0},{2,3},{3,2},{4,5},{5,4},{6,7},{7,6},{8,9},{9,8},{10,11... | collective-permute-start | bytes 2752520 | tf_op jit(solution)/shard_map/ppermute | solution.py:57
  245.1 2.5 collective-permute-start.28
  247.5 2.3 collective-permute-start.29
  249.9 5.7 %collective-permute-done.27 = bf16[128,896]{1,0:T(8,128)(2,1)S(1)} collective-permute-done((bf16[128,896]{1,0:T(8,128)(2,1)}, bf16[128,896]{1,0:T(8,128)(2,1)S(1)}, u32[]{:S(2)}, u32[]{:S(2)}) %collective-permute-start.27) | collective-permute-done | bytes 229408 | tf_op jit(solution)/shard_map/ppermute | solution.py:53
  255.6 8.0 %collective-permute-done.28 = bf16[128,896]{1,0:T(8,128)(2,1)S(1)} collective-permute-done((bf16[128,896]{1,0:T(8,128)(2,1)S(1)}, bf16[128,896]{1,0:T(8,128)(2,1)S(1)}, u32[]{:S(2)}, u32[]{:S(2)}) %collective-permute-start.28) | collective-permute-done | bytes 229408 | tf_op jit(solution)/shard_map/ppermute | solution.py:53
  263.6 7.3 %collective-permute-done.29 = bf16[128,896]{1,0:T(8,128)(2,1)} collective-permute-done((bf16[128,896]{1,0:T(8,128)(2,1)S(1)}, bf16[128,896]{1,0:T(8,128)(2,1)}, u32[]{:S(2)}, u32[]{:S(2)}) %collective-permute-start.29) | collective-permute-done | bytes 229408 | tf_op jit(solution)/shard_map/ppermute | solution.py:53
  270.8 1.9 fusion.3
  (100 shorter events, 27.1 us)
Async XLA Ops:
  0.0 42.2 %copy-start.20 = (f32[896]{0:T(1024)S(1)}, f32[896]{0:T(1024)}, u32[]{:S(2)}) copy-start(f32[896]{0:T(1024)} %param.15) | copy-start | bytes 10756
  0.0 52.2 %copy-start.15 = (bf16[128,896]{1,0:T(8,128)(2,1)S(1)}, bf16[128,896]{1,0:T(8,128)(2,1)}, u32[]{:S(2)}) copy-start(bf16[128,896]{1,0:T(8,128)(2,1)} %param.14) | copy-start | bytes 688132
  0.0 10.3 %collective-permute-start.8 = (bf16[112,896]{1,0:T(8,128)(2,1)}, bf16[112,896]{1,0:T(8,128)(2,1)S(1)}, u32[]{:S(2)}, u32[]{:S(2)}) collective-permute-start(bf16[112,896]{1,0:T(8,128)(2,1)} %param.13), channel_id=1, source_target_pairs={{0,128},{128,0},{1,129},{129,1},{2,130},{130,2},{3,131},{131,3},{4... | collective-permute-start | bytes 602120 | tf_op jit(solution)/shard_map/ppermute | solution.py:57
  2.5 12.1 %collective-permute-start = (bf16[448,128]{1,0:T(8,128)(2,1)}, bf16[448,128]{1,0:T(8,128)(2,1)S(1)}, u32[]{:S(2)}, u32[]{:S(2)}) collective-permute-start(bf16[448,128]{1,0:T(8,128)(2,1)} %bitcast.29), channel_id=1, source_target_pairs={{0,0},{1,32},{2,64},{3,96},{4,4},{5,36},{6,68},{7,100},{32,1},{33,... | collective-permute-start | bytes 344072 | tf_op jit(solution)/shard_map/ppermute | solution.py:110
  6.5 16.9 %collective-permute-start.1 = (bf16[448,128]{1,0:T(8,128)(2,1)}, bf16[448,128]{1,0:T(8,128)(2,1)S(1)}, u32[]{:S(2)}, u32[]{:S(2)}) collective-permute-start(bf16[448,128]{1,0:T(8,128)(2,1)} %bitcast.30), channel_id=1, source_target_pairs={{0,2},{1,34},{2,66},{3,98},{4,6},{5,38},{6,70},{7,102},{32,3},{33,... | collective-permute-start | bytes 344072 | tf_op jit(solution)/shard_map/ppermute | solution.py:110
  10.3 26.5 %collective-permute-start.10 = (bf16[224,896]{1,0:T(8,128)(2,1)S(1)}, bf16[224,896]{1,0:T(8,128)(2,1)S(1)}, u32[]{:S(2)}, u32[]{:S(2)}) collective-permute-start(bf16[224,896]{1,0:T(8,128)(2,1)S(1)} %constant_dynamic-update-slice_fusion.refs_8_), channel_id=1, source_target_pairs={{0,16},{8,24},{16,0},{24,8},{1,17},{9,25},{17,1},{25,9},{2,18},{10... | collective-permute-start | bytes 1204232 | tf_op jit(solution)/shard_map/ppermute | solution.py:53
  13.1 23.7 %collective-permute-start.11 = (bf16[224,896]{1,0:T(8,128)(2,1)S(1)}, bf16[224,896]{1,0:T(8,128)(2,1)S(1)}, u32[]{:S(2)}, u32[]{:S(2)}) collective-permute-start(bf16[224,896]{1,0:T(8,128)(2,1)S(1)} %constant_dynamic-update-slice_fusion.refs_8_), channel_id=1, source_target_pairs={{0,24},{8,0},{16,8},{24,16},{1,25},{9,1},{17,9},{25,17},{2,26},{10... | collective-permute-start | bytes 1204232 | tf_op jit(solution)/shard_map/ppermute | solution.py:53
  14.0 22.8 %collective-permute-start.9 = (bf16[224,896]{1,0:T(8,128)(2,1)S(1)}, bf16[224,896]{1,0:T(8,128)(2,1)S(1)}, u32[]{:S(2)}, u32[]{:S(2)}) collective-permute-start(bf16[224,896]{1,0:T(8,128)(2,1)S(1)} %constant_dynamic-update-slice_fusion.refs_8_), channel_id=1, source_target_pairs={{0,8},{8,16},{16,24},{24,0},{1,9},{9,17},{17,25},{25,1},{2,10},{10... | collective-permute-start | bytes 1204232 | tf_op jit(solution)/shard_map/ppermute | solution.py:53
  14.6 13.9 %collective-permute-start.2 = (bf16[448,128]{1,0:T(8,128)(2,1)}, bf16[448,128]{1,0:T(8,128)(2,1)S(1)}, u32[]{:S(2)}, u32[]{:S(2)}) collective-permute-start(bf16[448,128]{1,0:T(8,128)(2,1)} %bitcast.31), channel_id=1, source_target_pairs={{0,4},{1,36},{2,68},{3,100},{4,0},{5,32},{6,64},{7,96},{32,5},{33,... | collective-permute-start | bytes 344072 | tf_op jit(solution)/shard_map/ppermute | solution.py:110
  23.4 10.2 %collective-permute-start.3 = (bf16[448,128]{1,0:T(8,128)(2,1)}, bf16[448,128]{1,0:T(8,128)(2,1)S(1)}, u32[]{:S(2)}, u32[]{:S(2)}) collective-permute-start(bf16[448,128]{1,0:T(8,128)(2,1)} %bitcast.32), channel_id=1, source_target_pairs={{0,6},{1,38},{2,70},{3,102},{4,2},{5,34},{6,66},{7,98},{32,7},{33,... | collective-permute-start | bytes 344072 | tf_op jit(solution)/shard_map/ppermute | solution.py:110
  28.5 6.0 %collective-permute-start.4 = (bf16[448,128]{1,0:T(8,128)(2,1)S(1)}, bf16[448,128]{1,0:T(8,128)(2,1)S(1)}, u32[]{:S(2)}, u32[]{:S(2)}) collective-permute-start(bf16[448,128]{1,0:T(8,128)(2,1)S(1)} %collective-permute-done.refs_0_), channel_id=1, source_target_pairs={{0,1},{1,0},{2,3},{3,2},{4,5},{5,4},{6,7},{7,6},{8,9},{9,8},{10,11... | collective-permute-start | bytes 344072 | tf_op jit(solution)/shard_map/ppermute | solution.py:57
  33.6 1.8 collective-permute-start.5
  34.5 1.4 collective-permute-start.6
  35.5 1.3 collective-permute-start.7
  35.9 22.8 %copy-start.23 = (s32[128,2]{0,1:T(2,128)S(1)}, s32[128,2]{0,1:T(2,128)}, u32[]{:S(2)}) copy-start(s32[128,2]{0,1:T(2,128)} %param.16) | copy-start | bytes 3076
  35.9 22.8 %copy-start.22 = (s32[128,2]{0,1:T(2,128)S(1)}, s32[128,2]{0,1:T(2,128)}, u32[]{:S(2)}) copy-start(s32[128,2]{0,1:T(2,128)} %param.17) | copy-start | bytes 3076
  38.8 8.6 %collective-permute-start.12 = (bf16[128,896]{1,0:T(8,128)(2,1)S(1)}, bf16[128,896]{1,0:T(8,128)(2,1)S(1)}, u32[]{:S(2)}, u32[]{:S(2)}) collective-permute-start(bf16[128,896]{1,0:T(8,128)(2,1)S(1)} %get-tuple-element.39), channel_id=1, source_target_pairs={{0,32},{32,64},{64,96},{96,0},{1,33},{33,65},{65,97},{97,1},{2,34}... | collective-permute-start | bytes 688136 | tf_op jit(solution)/shard_map/ppermute | solution.py:53
  38.9 12.5 %collective-permute-start.13 = (bf16[128,896]{1,0:T(8,128)(2,1)S(1)}, bf16[128,896]{1,0:T(8,128)(2,1)S(1)}, u32[]{:S(2)}, u32[]{:S(2)}) collective-permute-start(bf16[128,896]{1,0:T(8,128)(2,1)S(1)} %get-tuple-element.40), channel_id=1, source_target_pairs={{0,64},{32,96},{64,0},{96,32},{1,65},{33,97},{65,1},{97,33},{2,66}... | collective-permute-start | bytes 688136 | tf_op jit(solution)/shard_map/ppermute | solution.py:53
  41.2 11.0 %collective-permute-start.14 = (bf16[128,896]{1,0:T(8,128)(2,1)S(1)}, bf16[128,896]{1,0:T(8,128)(2,1)S(1)}, u32[]{:S(2)}, u32[]{:S(2)}) collective-permute-start(bf16[128,896]{1,0:T(8,128)(2,1)S(1)} %get-tuple-element.41), channel_id=1, source_target_pairs={{0,96},{32,0},{64,32},{96,64},{1,97},{33,1},{65,33},{97,65},{2,98}... | collective-permute-start | bytes 688136 | tf_op jit(solution)/shard_map/ppermute | solution.py:53
  51.5 29.9 %copy-start.16 = (bf16[128,896]{1,0:T(8,128)(2,1)}, bf16[128,896]{1,0:T(8,128)(2,1)S(1)}, u32[]{:S(2)}) copy-start(bf16[128,896]{1,0:T(8,128)(2,1)S(1)} %collective-permute-done.13) | copy-start | bytes 688132
  52.2 36.2 %copy-start.18 = (bf16[128,896]{1,0:T(8,128)(2,1)}, bf16[128,896]{1,0:T(8,128)(2,1)S(1)}, u32[]{:S(2)}) copy-start(bf16[128,896]{1,0:T(8,128)(2,1)S(1)} %collective-permute-done.14) | copy-start | bytes 688132
  52.4 16.1 %collective-permute-start.15 = (bf16[136,896]{1,0:T(8,128)(2,1)S(1)}, bf16[136,896]{1,0:T(8,128)(2,1)S(1)}, u32[]{:S(2)}, u32[]{:S(2)}) collective-permute-start(bf16[136,896]{1,0:T(8,128)(2,1)S(1)} %pad_maximum_fusion.refs_0_), channel_id=1, source_target_pairs={{0,2},{2,4},{4,6},{6,0},{1,3},{3,5},{5,7},{7,1},{8,10},{10,12},{12... | collective-permute-start | bytes 731144 | tf_op jit(solution)/shard_map/ppermute | solution.py:53
  52.5 20.5 %collective-permute-start.16 = (bf16[136,896]{1,0:T(8,128)(2,1)S(1)}, bf16[136,896]{1,0:T(8,128)(2,1)S(1)}, u32[]{:S(2)}, u32[]{:S(2)}) collective-permute-start(bf16[136,896]{1,0:T(8,128)(2,1)S(1)} %pad_maximum_fusion.refs_0_), channel_id=1, source_target_pairs={{0,4},{2,6},{4,0},{6,2},{1,5},{3,7},{5,1},{7,3},{8,12},{10,14},{12... | collective-permute-start | bytes 731144 | tf_op jit(solution)/shard_map/ppermute | solution.py:53
  58.7 22.7 %collective-permute-start.17 = (bf16[136,896]{1,0:T(8,128)(2,1)S(1)}, bf16[136,896]{1,0:T(8,128)(2,1)S(1)}, u32[]{:S(2)}, u32[]{:S(2)}) collective-permute-start(bf16[136,896]{1,0:T(8,128)(2,1)S(1)} %pad_maximum_fusion.refs_0_), channel_id=1, source_target_pairs={{0,6},{2,0},{4,2},{6,4},{1,7},{3,1},{5,3},{7,5},{8,14},{10,8},{12,... | collective-permute-start | bytes 731144 | tf_op jit(solution)/shard_map/ppermute | solution.py:53
  58.8 24.7 %collective-permute-start.18 = (bf16[136,896]{1,0:T(8,128)(2,1)S(1)}, bf16[136,896]{1,0:T(8,128)(2,1)S(1)}, u32[]{:S(2)}, u32[]{:S(2)}) collective-permute-start(bf16[136,896]{1,0:T(8,128)(2,1)S(1)} %pad_maximum_fusion.refs_0_), channel_id=1, source_target_pairs={{0,1},{1,0},{2,3},{3,2},{4,5},{5,4},{6,7},{7,6},{8,9},{9,8},{10,11... | collective-permute-start | bytes 731144 | tf_op jit(solution)/shard_map/ppermute | solution.py:57
  68.5 14.9 %collective-permute-start.19 = (bf16[136,896]{1,0:T(8,128)(2,1)S(1)}, bf16[136,896]{1,0:T(8,128)(2,1)S(1)}, u32[]{:S(2)}, u32[]{:S(2)}) collective-permute-start(bf16[136,896]{1,0:T(8,128)(2,1)S(1)} %collective-permute-done.15.refs_1_), channel_id=1, source_target_pairs={{0,1},{1,0},{2,3},{3,2},{4,5},{5,4},{6,7},{7,6},{8,9},{9,8},{10,11... | collective-permute-start | bytes 731144 | tf_op jit(solution)/shard_map/ppermute | solution.py:57
  72.9 10.5 %collective-permute-start.20 = (bf16[136,896]{1,0:T(8,128)(2,1)S(1)}, bf16[136,896]{1,0:T(8,128)(2,1)S(1)}, u32[]{:S(2)}, u32[]{:S(2)}) collective-permute-start(bf16[136,896]{1,0:T(8,128)(2,1)S(1)} %collective-permute-done.16.refs_2_), channel_id=1, source_target_pairs={{0,1},{1,0},{2,3},{3,2},{4,5},{5,4},{6,7},{7,6},{8,9},{9,8},{10,11... | collective-permute-start | bytes 731144 | tf_op jit(solution)/shard_map/ppermute | solution.py:57
  81.4 2.4 collective-permute-start.21
  88.4 34.6 %all-to-all-start.2 = ((bf16[32,5,8,896]{3,2,1,0:T(8,128)(2,1)}), bf16[32,5,8,896]{3,2,1,0:T(8,128)(2,1)S(1)}, u32[]{:S(2)}, u32[]{:S(2)}) async-start(bf16[32,5,8,896]{3,2,1,0:T(8,128)(2,1)} %get-tuple-element.56), calls=%async_computation.2 | async-start | bytes 4587520 | tf_op jit(solution)/shard_map/all_to_all | solution.py:374
  94.2 7.1 %collective-permute-start.22 = (bf16[7168,256]{1,0:T(8,128)(2,1)}, bf16[7168,256]{1,0:T(8,128)(2,1)S(1)}, u32[]{:S(2)}, u32[]{:S(2)}) collective-permute-start(bf16[7168,256]{1,0:T(8,128)(2,1)} %bitcast.19), channel_id=1, source_target_pairs={{0,1},{1,0},{2,3},{3,2},{4,5},{5,4},{6,7},{7,6},{8,9},{9,8},{10,11... | collective-permute-start | bytes 11010056 | tf_op jit(solution)/shard_map/ppermute | solution.py:57
  94.9 16.7 %collective-permute-start.23 = (bf16[7168,256]{1,0:T(8,128)(2,1)}, bf16[7168,256]{1,0:T(8,128)(2,1)S(1)}, u32[]{:S(2)}, u32[]{:S(2)}) collective-permute-start(bf16[7168,256]{1,0:T(8,128)(2,1)} %bitcast.22), channel_id=1, source_target_pairs={{0,1},{1,0},{2,3},{3,2},{4,5},{5,4},{6,7},{7,6},{8,9},{9,8},{10,11... | collective-permute-start | bytes 11010056 | tf_op jit(solution)/shard_map/ppermute | solution.py:57
  95.0 18.5 %collective-permute-start.24 = (bf16[256,7168]{1,0:T(8,128)(2,1)}, bf16[256,7168]{1,0:T(8,128)(2,1)}, u32[]{:S(2)}, u32[]{:S(2)}) collective-permute-start(bf16[256,7168]{1,0:T(8,128)(2,1)} %bitcast.25), channel_id=1, source_target_pairs={{0,1},{1,0},{2,3},{3,2},{4,5},{5,4},{6,7},{7,6},{8,9},{9,8},{10,11... | collective-permute-start | bytes 11010056 | tf_op jit(solution)/shard_map/ppermute | solution.py:57
  123.0 35.4 %all-to-all-start = ((bf16[32,5,8,896]{3,2,1,0:T(8,128)(2,1)}), bf16[32,5,8,896]{3,2,1,0:T(8,128)(2,1)}, u32[]{:S(2)}, u32[]{:S(2)}) async-start(bf16[32,5,8,896]{3,2,1,0:T(8,128)(2,1)} %shard_map.102), calls=%async_computation | async-start | bytes 4587520 | tf_op jit(solution)/shard_map/all_to_all | solution.py:374
  130.2 2.0 copy-start
  132.2 2.0 copy-start.2
  134.3 2.0 copy-start.4
  158.4 36.1 %all-to-all-start.3 = ((bf16[32,5,8,896]{3,2,1,0:T(8,128)(2,1)}), bf16[32,5,8,896]{3,2,1,0:T(8,128)(2,1)S(1)}, u32[]{:S(2)}, u32[]{:S(2)}) async-start(bf16[32,5,8,896]{3,2,1,0:T(8,128)(2,1)} %shard_map.105), calls=%async_computation.3 | async-start | bytes 4587520 | tf_op jit(solution)/shard_map/all_to_all | solution.py:376
  165.8 2.0 copy-start.1
  187.9 14.0 %copy-start.21 = (f32[128,2]{0,1:T(2,128)S(1)}, f32[128,2]{0,1:T(2,128)}, u32[]{:S(2)}) copy-start(f32[128,2]{0,1:T(2,128)} %param.18) | copy-start | bytes 3076
  194.5 36.0 %all-to-all-start.1 = ((bf16[32,5,8,896]{3,2,1,0:T(8,128)(2,1)}), bf16[32,5,8,896]{3,2,1,0:T(8,128)(2,1)}, u32[]{:S(2)}, u32[]{:S(2)}) async-start(bf16[32,5,8,896]{3,2,1,0:T(8,128)(2,1)} %shard_map.103), calls=%async_computation.1 | async-start | bytes 4587520 | tf_op jit(solution)/shard_map/all_to_all | solution.py:376
  207.1 32.1 %copy-start.14 = (bf16[4,128,896]{2,1,0:T(8,128)(2,1)S(1)}, bf16[4,128,896]{2,1,0:T(8,128)(2,1)}, u32[]{:S(2)}) copy-start(bf16[4,128,896]{2,1,0:T(8,128)(2,1)} %copy-done.13) | copy-start | bytes 2752516
  207.1 32.1 %collective-permute-start.26 = (bf16[4,128,896]{2,1,0:T(8,128)(2,1)}, bf16[4,128,896]{2,1,0:T(8,128)(2,1)}, u32[]{:S(2)}, u32[]{:S(2)}) collective-permute-start(bf16[4,128,896]{2,1,0:T(8,128)(2,1)} %get-tuple-element.58), channel_id=1, source_target_pairs={{0,1},{1,0},{2,3},{3,2},{4,5},{5,4},{6,7},{7,6},{8,9},{9,8},{10,11... | collective-permute-start | bytes 2752520 | tf_op jit(solution)/shard_map/ppermute | solution.py:57
  235.7 5.9 %collective-permute-start.25 = (bf16[4,128,896]{2,1,0:T(8,128)(2,1)}, bf16[4,128,896]{2,1,0:T(8,128)(2,1)}, u32[]{:S(2)}, u32[]{:S(2)}) collective-permute-start(bf16[4,128,896]{2,1,0:T(8,128)(2,1)} %get-tuple-element.55), channel_id=1, source_target_pairs={{0,1},{1,0},{2,3},{3,2},{4,5},{5,4},{6,7},{7,6},{8,9},{9,8},{10,11... | collective-permute-start | bytes 2752520 | tf_op jit(solution)/shard_map/ppermute | solution.py:57
  241.6 29.2 %copy-start.17 = (bf16[128,896]{1,0:T(8,128)(2,1)S(1)}, bf16[128,896]{1,0:T(8,128)(2,1)}, u32[]{:S(2)}) copy-start(bf16[128,896]{1,0:T(8,128)(2,1)} %copy-done.16) | copy-start | bytes 688132
  241.6 29.2 %copy-start.19 = (bf16[128,896]{1,0:T(8,128)(2,1)S(1)}, bf16[128,896]{1,0:T(8,128)(2,1)}, u32[]{:S(2)}) copy-start(bf16[128,896]{1,0:T(8,128)(2,1)} %copy-done.18) | copy-start | bytes 688132
  244.0 11.6 %collective-permute-start.27 = (bf16[128,896]{1,0:T(8,128)(2,1)}, bf16[128,896]{1,0:T(8,128)(2,1)S(1)}, u32[]{:S(2)}, u32[]{:S(2)}) collective-permute-start(bf16[128,896]{1,0:T(8,128)(2,1)} %get-tuple-element.61), channel_id=1, source_target_pairs={{0,2},{2,4},{4,6},{6,0},{1,3},{3,5},{5,7},{7,1},{8,10},{10,12},{12... | collective-permute-start | bytes 688136 | tf_op jit(solution)/shard_map/ppermute | solution.py:53
  245.1 18.5 %collective-permute-start.28 = (bf16[128,896]{1,0:T(8,128)(2,1)S(1)}, bf16[128,896]{1,0:T(8,128)(2,1)S(1)}, u32[]{:S(2)}, u32[]{:S(2)}) collective-permute-start(bf16[128,896]{1,0:T(8,128)(2,1)S(1)} %get-tuple-element.63), channel_id=1, source_target_pairs={{0,4},{2,6},{4,0},{6,2},{1,5},{3,7},{5,1},{7,3},{8,12},{10,14},{12... | collective-permute-start | bytes 688136 | tf_op jit(solution)/shard_map/ppermute | solution.py:53
  247.5 23.3 %collective-permute-start.29 = (bf16[128,896]{1,0:T(8,128)(2,1)S(1)}, bf16[128,896]{1,0:T(8,128)(2,1)}, u32[]{:S(2)}, u32[]{:S(2)}) collective-permute-start(bf16[128,896]{1,0:T(8,128)(2,1)S(1)} %get-tuple-element.62), channel_id=1, source_target_pairs={{0,6},{2,0},{4,2},{6,4},{1,7},{3,1},{5,3},{7,5},{8,14},{10,8},{12,... | collective-permute-start | bytes 688136 | tf_op jit(solution)/shard_map/ppermute | solution.py:53
  (10 other events, 18.4 us)
where the time goes:
time: 274 us; the launch traced here: 273 us
  waiting for transfers between devices  111 us (41%)
  starting transfers between devices  85.6 us (31%)
  Pallas kernels  41.7 us (15%)
  local copies, waits for them, and re-layouts  29.2 us (11%)
  other arithmetic  5.14 us (2%)
    ppermute x12, waiting for transfers between devices, shift(): lax.ppermute(value, axis, [(i, (i + step) % size) for i in range(size)])  42 us
    all_to_all x2, waiting for transfers between devices, shards(): lax.all_to_all(half_out, EXPERT, split_axis=0, concat_axis=0, tiled=True)  28.8 us
    unnamed x50, local copies, waits for them, and re-layouts  27.6 us
    pallas_call x2, Pallas kernels, experts(): call(experts_kernel, SLAB_SHAPE, 2 * SLOTS * D * HID * 6, 27000000, 34, g...  22.9 us
    ppermute x14, starting transfers between devices, swap(): return lax.ppermute(value, axis, [(0, 1), (1, 0)])  22.2 us
    ppermute x12, starting transfers between devices, shift(): lax.ppermute(value, axis, [(i, (i + step) % size) for i in range(size)])  19.9 us
    all_to_all x2, waiting for transfers between devices, shards(): lax.all_to_all(rows, EXPERT, split_axis=0, concat_axis=0, tiled=True)  16.5 us
    ppermute x4, starting transfers between devices, project(): features.append(lax.ppermute(flipped, ('y',) + MP, pairs))  15.7 us
  transfers between devices with their start and end apart: 34, of which 21 were waited for; matrix products, arithmetic and copies ran while one was open for 1% of the time, Pallas kernels for 13%

commit v1 on v0

--- a/solution.py
+++ b/solution.py
@@ -329,6 +329,7 @@
         (shape, shape),
         2_500_000_000,
         6_000_000,
+        14,
         grid=(NZ,),
         in_specs=[SMEM, whole((TOK, 2)), whole((TOK, 2)), whole(SLAB)],
         out_specs=[pl.BlockSpec((1, TOK, SHARD), lambda step: (step, 0, 0))] * 2,
@@ -366,7 +367,9 @@
 
     hidden_state = project(place, attention, out_weight, residual)
     one, two = dispatch(place, codes.T, hidden_state, norm_gain)
-    one, gate, up, down = lax.optimization_barrier((one, w_gate[0], w_up[0], w_down[0]))
+    one, hidden_state, gate, up, down = lax.optimization_barrier(
+        (one, hidden_state, w_gate[0], w_up[0], w_down[0])
+    )
     gate, up, down = [(value, swap(value, "core")) for value in (gate, up, down)]
     two, gate, up, down = lax.optimization_barrier((two, gate, up, down))
     returned = []

time: 274 us -> 272 us (level)
    unnamed x50 -> x40, local copies, waits for them, and re-layouts: 27.6 us -> 26.6 us
where the time goes in v1:
time: 272 us; the launch traced here: 271 us
  waiting for transfers between devices  112 us (41%)
  starting transfers between devices  85.8 us (32%)
  Pallas kernels  40.6 us (15%)
  local copies, waits for them, and re-layouts  27.5 us (10%)
  other arithmetic  4.8 us (2%)
    ppermute x12, waiting for transfers between devices, shift(): lax.ppermute(value, axis, [(i, (i + step) % size) for i in range(size)])  41.9 us
    all_to_all x2, waiting for transfers between devices, shards(): lax.all_to_all(half_out, EXPERT, split_axis=0, concat_axis=0, tiled=True)  29.9 us
    unnamed x40, local copies, waits for them, and re-layouts  26.6 us
    pallas_call x2, Pallas kernels, experts(): call(experts_kernel, SLAB_SHAPE, 2 * SLOTS * D * HID * 6, 27000000, 34, g...  22.9 us
    ppermute x14, starting transfers between devices, swap(): return lax.ppermute(value, axis, [(0, 1), (1, 0)])  22.3 us
    ppermute x12, starting transfers between devices, shift(): lax.ppermute(value, axis, [(i, (i + step) % size) for i in range(size)])  20 us
    all_to_all x2, waiting for transfers between devices, shards(): lax.all_to_all(rows, EXPERT, split_axis=0, concat_axis=0, tiled=True)  16.5 us
    ppermute x4, starting transfers between devices, project(): features.append(lax.ppermute(flipped, ('y',) + MP, pairs))  15.7 us
  transfers between devices with their start and end apart: 34, of which 21 were waited for; matrix products, arithmetic and copies ran while one was open for 1% of the time, Pallas kernels for 13%

profile of v1, /device:TPU:1, one launch (start us, length us, event | category | flops | bytes accessed | tf_op | source)
XLA Modules:
  0.0 270.6 jit_solution(6615907498174682650)
XLA Ops:
  0.0 2.5 collective-permute-start.8
  2.5 4.0 %collective-permute-start = (bf16[448,128]{1,0:T(8,128)(2,1)}, bf16[448,128]{1,0:T(8,128)(2,1)S(1)}, u32[]{:S(2)}, u32[]{:S(2)}) collective-permute-start(bf16[448,128]{1,0:T(8,128)(2,1)} %bitcast.29), channel_id=1, source_target_pairs={{0,0},{1,32},{2,64},{3,96},{4,4},{5,36},{6,68},{7,100},{32,1},{33,... | collective-permute-start | bytes 344072 | tf_op jit(solution)/shard_map/ppermute | solution.py:110
  6.5 2.8 %collective-permute-start.1 = (bf16[448,128]{1,0:T(8,128)(2,1)}, bf16[448,128]{1,0:T(8,128)(2,1)S(1)}, u32[]{:S(2)}, u32[]{:S(2)}) collective-permute-start(bf16[448,128]{1,0:T(8,128)(2,1)} %bitcast.30), channel_id=1, source_target_pairs={{0,2},{1,34},{2,66},{3,98},{4,6},{5,38},{6,70},{7,102},{32,3},{33,... | collective-permute-start | bytes 344072 | tf_op jit(solution)/shard_map/ppermute | solution.py:110
  10.3 2.8 %collective-permute-start.10 = (bf16[224,896]{1,0:T(8,128)(2,1)S(1)}, bf16[224,896]{1,0:T(8,128)(2,1)S(1)}, u32[]{:S(2)}, u32[]{:S(2)}) collective-permute-start(bf16[224,896]{1,0:T(8,128)(2,1)S(1)} %constant_dynamic-update-slice_fusion.refs_8_), channel_id=1, source_target_pairs={{0,16},{8,24},{16,0},{24,8},{1,17},{9,25},{17,1},{25,9},{2,18},{10... | collective-permute-start | bytes 1204232 | tf_op jit(solution)/shard_map/ppermute | solution.py:53
  14.6 8.8 %collective-permute-start.2 = (bf16[448,128]{1,0:T(8,128)(2,1)}, bf16[448,128]{1,0:T(8,128)(2,1)S(1)}, u32[]{:S(2)}, u32[]{:S(2)}) collective-permute-start(bf16[448,128]{1,0:T(8,128)(2,1)} %bitcast.31), channel_id=1, source_target_pairs={{0,4},{1,36},{2,68},{3,100},{4,0},{5,32},{6,64},{7,96},{32,5},{33,... | collective-permute-start | bytes 344072 | tf_op jit(solution)/shard_map/ppermute | solution.py:110
  23.4 5.1 %collective-permute-done.2.refs_2_ = bf16[448,128]{1,0:T(8,128)(2,1)S(1)} collective-permute-done((bf16[448,128]{1,0:T(8,128)(2,1)}, bf16[448,128]{1,0:T(8,128)(2,1)S(1)}, u32[]{:S(2)}, u32[]{:S(2)}) %collective-permute-start.2) | collective-permute-done | bytes 114720 | tf_op jit(solution)/shard_map/ppermute | solution.py:110
  28.5 5.1 %collective-permute-done.3.refs_3_ = bf16[448,128]{1,0:T(8,128)(2,1)S(1)} collective-permute-done((bf16[448,128]{1,0:T(8,128)(2,1)}, bf16[448,128]{1,0:T(8,128)(2,1)S(1)}, u32[]{:S(2)}, u32[]{:S(2)}) %collective-permute-start.3) | collective-permute-done | bytes 114720 | tf_op jit(solution)/shard_map/ppermute | solution.py:110
  36.8 2.0 shard_map.100
  38.9 2.2 collective-permute-start.13
  42.3 5.1 %collective-permute-done.12 = bf16[128,896]{1,0:T(8,128)(2,1)S(1)} collective-permute-done((bf16[128,896]{1,0:T(8,128)(2,1)S(1)}, bf16[128,896]{1,0:T(8,128)(2,1)S(1)}, u32[]{:S(2)}, u32[]{:S(2)}) %collective-permute-start.12) | collective-permute-done | bytes 229408 | tf_op jit(solution)/shard_map/ppermute | solution.py:53
  47.4 4.1 %collective-permute-done.13 = bf16[128,896]{1,0:T(8,128)(2,1)S(1)} collective-permute-done((bf16[128,896]{1,0:T(8,128)(2,1)S(1)}, bf16[128,896]{1,0:T(8,128)(2,1)S(1)}, u32[]{:S(2)}, u32[]{:S(2)}) %collective-permute-start.13) | collective-permute-done | bytes 229408 | tf_op jit(solution)/shard_map/ppermute | solution.py:53
  53.2 6.3 %collective-permute-start.16 = (bf16[136,896]{1,0:T(8,128)(2,1)S(1)}, bf16[136,896]{1,0:T(8,128)(2,1)S(1)}, u32[]{:S(2)}, u32[]{:S(2)}) collective-permute-start(bf16[136,896]{1,0:T(8,128)(2,1)S(1)} %pad_maximum_fusion.refs_0_), channel_id=1, source_target_pairs={{0,4},{2,6},{4,0},{6,2},{1,5},{3,7},{5,1},{7,3},{8,12},{10,14},{12... | collective-permute-start | bytes 731144 | tf_op jit(solution)/shard_map/ppermute | solution.py:53
  59.5 2.2 collective-permute-start.18
  61.7 7.6 %collective-permute-done.15.refs_1_ = bf16[136,896]{1,0:T(8,128)(2,1)S(1)} collective-permute-done((bf16[136,896]{1,0:T(8,128)(2,1)S(1)}, bf16[136,896]{1,0:T(8,128)(2,1)S(1)}, u32[]{:S(2)}, u32[]{:S(2)}) %collective-permute-start.15) | collective-permute-done | bytes 243744 | tf_op jit(solution)/shard_map/ppermute | solution.py:53
  70.1 3.6 %collective-permute-done.16.refs_2_ = bf16[136,896]{1,0:T(8,128)(2,1)S(1)} collective-permute-done((bf16[136,896]{1,0:T(8,128)(2,1)S(1)}, bf16[136,896]{1,0:T(8,128)(2,1)S(1)}, u32[]{:S(2)}, u32[]{:S(2)}) %collective-permute-start.16) | collective-permute-done | bytes 243744 | tf_op jit(solution)/shard_map/ppermute | solution.py:53
  73.7 8.4 %collective-permute-start.20 = (bf16[136,896]{1,0:T(8,128)(2,1)S(1)}, bf16[136,896]{1,0:T(8,128)(2,1)S(1)}, u32[]{:S(2)}, u32[]{:S(2)}) collective-permute-start(bf16[136,896]{1,0:T(8,128)(2,1)S(1)} %collective-permute-done.16.refs_2_), channel_id=1, source_target_pairs={{0,1},{1,0},{2,3},{3,2},{4,5},{5,4},{6,7},{7,6},{8,9},{9,8},{10,11... | collective-permute-start | bytes 731144 | tf_op jit(solution)/shard_map/ppermute | solution.py:57
  84.5 4.5 %shard_map.101 = (bf16[8,128,896]{2,1,0:T(8,128)(2,1)}, bf16[32,5,8,896]{3,2,1,0:T(8,128)(2,1)}) custom-call(s32[5]{0:T(128)S(1)} %stack.39.place, s32[2,128]{1,0:T(2,128)S(1)} %copy.30.codes, bf16[136,896]{1,0:T(8,128)(2,1)S(1)} %pad_maximum_fusion.refs_0_, bf16[136,896]{1,0:T(8,128)(2,1)S(1)} %collective-permute-done.15.refs_1_, ...), custom_call_target="tpu_custom_call" | custom-call | flops 2000000000 | bytes 6000000 | tf_op jit(solution)/shard_map/pallas_call | solution.py:220
  89.1 5.8 %all-to-all-start.2 = ((bf16[32,5,8,896]{3,2,1,0:T(8,128)(2,1)}), bf16[32,5,8,896]{3,2,1,0:T(8,128)(2,1)S(1)}, u32[]{:S(2)}, u32[]{:S(2)}) async-start(bf16[32,5,8,896]{3,2,1,0:T(8,128)(2,1)} %get-tuple-element.58), calls=%async_computation.2 | async-start | bytes 4587520 | tf_op jit(solution)/shard_map/all_to_all | solution.py:377
  97.6 2.8 %shard_map.102 = bf16[32,5,8,896]{3,2,1,0:T(8,128)(2,1)} custom-call(s32[2,128]{1,0:T(2,128)S(1)} %copy.30.codes, bf16[8,128,896]{2,1,0:T(8,128)(2,1)S(1)} %copy-done.12), custom_call_target="tpu_custom_call" | custom-call | flops 1000000000 | bytes 4000000 | tf_op jit(solution)/shard_map/pallas_call | solution.py:230
  103.8 8.6 %collective-permute-done.23.up_b = bf16[7168,256]{1,0:T(8,128)(2,1)S(1)} collective-permute-done((bf16[7168,256]{1,0:T(8,128)(2,1)}, bf16[7168,256]{1,0:T(8,128)(2,1)S(1)}, u32[]{:S(2)}, u32[]{:S(2)}) %collective-permute-start.23) | collective-permute-done | bytes 3670048 | tf_op jit(solution)/shard_map/ppermute | solution.py:57
  112.4 1.9 copy-done.9
  114.2 9.5 %all-to-all-done.2.units = bf16[32,5,8,896]{3,2,1,0:T(8,128)(2,1)S(1)} async-done(((bf16[32,5,8,896]{3,2,1,0:T(8,128)(2,1)}), bf16[32,5,8,896]{3,2,1,0:T(8,128)(2,1)S(1)}, u32[]{:S(2)}, u32[]{:S(2)}) %all-to-all-start.2) | async-done | bytes 2293792 | tf_op jit(solution)/shard_map/all_to_all | solution.py:377
  123.7 7.2 %all-to-all-start = ((bf16[32,5,8,896]{3,2,1,0:T(8,128)(2,1)}), bf16[32,5,8,896]{3,2,1,0:T(8,128)(2,1)}, u32[]{:S(2)}, u32[]{:S(2)}) async-start(bf16[32,5,8,896]{3,2,1,0:T(8,128)(2,1)} %shard_map.102), calls=%async_computation | async-start | bytes 4587520 | tf_op jit(solution)/shard_map/all_to_all | solution.py:377
  130.9 2.0 copy-done
  132.9 2.0 copy-done.2
  135.0 2.0 copy-done.4
  137.0 2.0 copy-done.7
  139.0 2.0 copy-done.10
  141.1 11.0 %shard_map.105 = bf16[32,5,8,896]{3,2,1,0:T(8,128)(2,1)} custom-call(bf16[32,5,8,896]{3,2,1,0:T(8,128)(2,1)S(1)} %all-to-all-done.2.units, bf16[7168,256]{1,0:T(8,128)(2,1)S(1)} %bitcast.20, bf16[7168,256]{1,0:T(8,128)(2,1)S(1)} %bitcast.23, bf16[7168,256]{1,0:T(8,128)(2,1)S(1)} %copy-done.7, bf16[7168,256]{1,0:T(8,128)(2,1)S(1)} %copy-done.10, ...), custom_call_target="tpu_custom_call" | custom-call | flops 3523215360 | bytes 27000000 | tf_op jit(solution)/shard_map/pallas_call | solution.py:279
  152.1 7.0 %all-to-all-done.units = bf16[32,5,8,896]{3,2,1,0:T(8,128)(2,1)} async-done(((bf16[32,5,8,896]{3,2,1,0:T(8,128)(2,1)}), bf16[32,5,8,896]{3,2,1,0:T(8,128)(2,1)}, u32[]{:S(2)}, u32[]{:S(2)}) %all-to-all-start) | async-done | bytes 2293792 | tf_op jit(solution)/shard_map/all_to_all | solution.py:377
  159.1 7.4 %all-to-all-start.3 = ((bf16[32,5,8,896]{3,2,1,0:T(8,128)(2,1)}), bf16[32,5,8,896]{3,2,1,0:T(8,128)(2,1)S(1)}, u32[]{:S(2)}, u32[]{:S(2)}) async-start(bf16[32,5,8,896]{3,2,1,0:T(8,128)(2,1)} %shard_map.105), calls=%async_computation.3 | async-start | bytes 4587520 | tf_op jit(solution)/shard_map/all_to_all | solution.py:379
  166.5 2.0 copy-done.1
  168.6 2.0 copy-done.3
  170.6 2.0 copy-done.5
  172.7 2.0 copy-done.8
  174.7 2.0 copy-done.11
  176.7 11.9 %shard_map.103 = bf16[32,5,8,896]{3,2,1,0:T(8,128)(2,1)} custom-call(bf16[32,5,8,896]{3,2,1,0:T(8,128)(2,1)} %all-to-all-done.units, bf16[7168,256]{1,0:T(8,128)(2,1)S(1)} %bitcast.21, bf16[7168,256]{1,0:T(8,128)(2,1)S(1)} %bitcast.24, bf16[7168,256]{1,0:T(8,128)(2,1)S(1)} %copy-done.8, bf16[7168,256]{1,0:T(8,128)(2,1)S(1)} %copy-done.11, ...), custom_call_target="tpu_custom_call" | custom-call | flops 3523215360 | bytes 27000000 | tf_op jit(solution)/shard_map/pallas_call | solution.py:279
  188.6 6.6 %all-to-all-done.3.units = bf16[32,5,8,896]{3,2,1,0:T(8,128)(2,1)S(1)} async-done(((bf16[32,5,8,896]{3,2,1,0:T(8,128)(2,1)}), bf16[32,5,8,896]{3,2,1,0:T(8,128)(2,1)S(1)}, u32[]{:S(2)}, u32[]{:S(2)}) %all-to-all-start.3) | async-done | bytes 2293792 | tf_op jit(solution)/shard_map/all_to_all | solution.py:379
  195.2 7.3 %all-to-all-start.1 = ((bf16[32,5,8,896]{3,2,1,0:T(8,128)(2,1)}), bf16[32,5,8,896]{3,2,1,0:T(8,128)(2,1)}, u32[]{:S(2)}, u32[]{:S(2)}) async-start(bf16[32,5,8,896]{3,2,1,0:T(8,128)(2,1)} %shard_map.103), calls=%async_computation.1 | async-start | bytes 4587520 | tf_op jit(solution)/shard_map/all_to_all | solution.py:379
  202.6 4.1 %shard_map.106 = (bf16[4,128,896]{2,1,0:T(8,128)(2,1)S(1)}, bf16[4,128,896]{2,1,0:T(8,128)(2,1)}) custom-call(s32[5]{0:T(128)S(1)} %stack.39.place, s32[128,2]{1,0:T(8,128)S(1)} %add_select_fusion.codes, f32[128,2]{1,0:T(8,128)S(1)} %copy.32.probs, bf16[32,5,8,896]{3,2,1,0:T(8,128)(2,1)S(1)} %all-to-all-done.3.units), custom_call_target="tpu_custom_call" | custom-call | flops 2500000000 | bytes 6000000 | tf_op jit(solution)/shard_map/pallas_call | solution.py:327
  207.9 23.3 %all-to-all-done.1.units = bf16[32,5,8,896]{3,2,1,0:T(8,128)(2,1)} async-done(((bf16[32,5,8,896]{3,2,1,0:T(8,128)(2,1)}), bf16[32,5,8,896]{3,2,1,0:T(8,128)(2,1)}, u32[]{:S(2)}, u32[]{:S(2)}) %all-to-all-start.1) | async-done | bytes 2293792 | tf_op jit(solution)/shard_map/all_to_all | solution.py:379
  231.1 4.3 %shard_map.104 = (bf16[4,128,896]{2,1,0:T(8,128)(2,1)S(1)}, bf16[4,128,896]{2,1,0:T(8,128)(2,1)S(1)}) custom-call(s32[5]{0:T(128)S(1)} %stack.39.place, s32[128,2]{1,0:T(8,128)S(1)} %add_select_fusion.codes, f32[128,2]{1,0:T(8,128)S(1)} %copy.32.probs, bf16[32,5,8,896]{3,2,1,0:T(8,128)(2,1)} %all-to-all-done.1.units), custom_call_target="tpu_custom_call" | custom-call | flops 2500000000 | bytes 6000000 | tf_op jit(solution)/shard_map/pallas_call | solution.py:327
  235.5 3.6 %collective-permute-start.25 = (bf16[4,128,896]{2,1,0:T(8,128)(2,1)S(1)}, bf16[4,128,896]{2,1,0:T(8,128)(2,1)}, u32[]{:S(2)}, u32[]{:S(2)}) collective-permute-start(bf16[4,128,896]{2,1,0:T(8,128)(2,1)S(1)} %get-tuple-element.57), channel_id=1, source_target_pairs={{0,1},{1,0},{2,3},{3,2},{4,5},{5,4},{6,7},{7,6},{8,9},{9,8},{10,11... | collective-permute-start | bytes 2752520 | tf_op jit(solution)/shard_map/ppermute | solution.py:57
  244.1 2.5 collective-permute-start.28
  246.6 2.3 collective-permute-start.29
  248.9 5.6 %collective-permute-done.27 = bf16[128,896]{1,0:T(8,128)(2,1)S(1)} collective-permute-done((bf16[128,896]{1,0:T(8,128)(2,1)S(1)}, bf16[128,896]{1,0:T(8,128)(2,1)S(1)}, u32[]{:S(2)}, u32[]{:S(2)}) %collective-permute-start.27) | collective-permute-done | bytes 229408 | tf_op jit(solution)/shard_map/ppermute | solution.py:53
  254.6 8.0 %collective-permute-done.28 = bf16[128,896]{1,0:T(8,128)(2,1)S(1)} collective-permute-done((bf16[128,896]{1,0:T(8,128)(2,1)S(1)}, bf16[128,896]{1,0:T(8,128)(2,1)S(1)}, u32[]{:S(2)}, u32[]{:S(2)}) %collective-permute-start.28) | collective-permute-done | bytes 229408 | tf_op jit(solution)/shard_map/ppermute | solution.py:53
  262.6 7.2 %collective-permute-done.29 = bf16[128,896]{1,0:T(8,128)(2,1)S(1)} collective-permute-done((bf16[128,896]{1,0:T(8,128)(2,1)S(1)}, bf16[128,896]{1,0:T(8,128)(2,1)S(1)}, u32[]{:S(2)}, u32[]{:S(2)}) %collective-permute-start.29) | collective-permute-done | bytes 229408 | tf_op jit(solution)/shard_map/ppermute | solution.py:53
  (90 shorter events, 25.0 us)
Async XLA Ops:
  0.0 42.2 %copy-start.15 = (f32[896]{0:T(1024)S(1)}, f32[896]{0:T(1024)}, u32[]{:S(2)}) copy-start(f32[896]{0:T(1024)} %param.15) | copy-start | bytes 10756
  0.0 52.2 %copy-start.14 = (bf16[128,896]{1,0:T(8,128)(2,1)S(1)}, bf16[128,896]{1,0:T(8,128)(2,1)}, u32[]{:S(2)}) copy-start(bf16[128,896]{1,0:T(8,128)(2,1)} %param.14) | copy-start | bytes 688132
  0.0 10.3 %collective-permute-start.8 = (bf16[112,896]{1,0:T(8,128)(2,1)}, bf16[112,896]{1,0:T(8,128)(2,1)S(1)}, u32[]{:S(2)}, u32[]{:S(2)}) collective-permute-start(bf16[112,896]{1,0:T(8,128)(2,1)} %param.13), channel_id=1, source_target_pairs={{0,128},{128,0},{1,129},{129,1},{2,130},{130,2},{3,131},{131,3},{4... | collective-permute-start | bytes 602120 | tf_op jit(solution)/shard_map/ppermute | solution.py:57
  2.5 12.1 %collective-permute-start = (bf16[448,128]{1,0:T(8,128)(2,1)}, bf16[448,128]{1,0:T(8,128)(2,1)S(1)}, u32[]{:S(2)}, u32[]{:S(2)}) collective-permute-start(bf16[448,128]{1,0:T(8,128)(2,1)} %bitcast.29), channel_id=1, source_target_pairs={{0,0},{1,32},{2,64},{3,96},{4,4},{5,36},{6,68},{7,100},{32,1},{33,... | collective-permute-start | bytes 344072 | tf_op jit(solution)/shard_map/ppermute | solution.py:110
  6.5 16.9 %collective-permute-start.1 = (bf16[448,128]{1,0:T(8,128)(2,1)}, bf16[448,128]{1,0:T(8,128)(2,1)S(1)}, u32[]{:S(2)}, u32[]{:S(2)}) collective-permute-start(bf16[448,128]{1,0:T(8,128)(2,1)} %bitcast.30), channel_id=1, source_target_pairs={{0,2},{1,34},{2,66},{3,98},{4,6},{5,38},{6,70},{7,102},{32,3},{33,... | collective-permute-start | bytes 344072 | tf_op jit(solution)/shard_map/ppermute | solution.py:110
  10.3 26.5 %collective-permute-start.10 = (bf16[224,896]{1,0:T(8,128)(2,1)S(1)}, bf16[224,896]{1,0:T(8,128)(2,1)S(1)}, u32[]{:S(2)}, u32[]{:S(2)}) collective-permute-start(bf16[224,896]{1,0:T(8,128)(2,1)S(1)} %constant_dynamic-update-slice_fusion.refs_8_), channel_id=1, source_target_pairs={{0,16},{8,24},{16,0},{24,8},{1,17},{9,25},{17,1},{25,9},{2,18},{10... | collective-permute-start | bytes 1204232 | tf_op jit(solution)/shard_map/ppermute | solution.py:53
  13.1 23.7 %collective-permute-start.11 = (bf16[224,896]{1,0:T(8,128)(2,1)S(1)}, bf16[224,896]{1,0:T(8,128)(2,1)S(1)}, u32[]{:S(2)}, u32[]{:S(2)}) collective-permute-start(bf16[224,896]{1,0:T(8,128)(2,1)S(1)} %constant_dynamic-update-slice_fusion.refs_8_), channel_id=1, source_target_pairs={{0,24},{8,0},{16,8},{24,16},{1,25},{9,1},{17,9},{25,17},{2,26},{10... | collective-permute-start | bytes 1204232 | tf_op jit(solution)/shard_map/ppermute | solution.py:53
  14.0 22.8 %collective-permute-start.9 = (bf16[224,896]{1,0:T(8,128)(2,1)S(1)}, bf16[224,896]{1,0:T(8,128)(2,1)S(1)}, u32[]{:S(2)}, u32[]{:S(2)}) collective-permute-start(bf16[224,896]{1,0:T(8,128)(2,1)S(1)} %constant_dynamic-update-slice_fusion.refs_8_), channel_id=1, source_target_pairs={{0,8},{8,16},{16,24},{24,0},{1,9},{9,17},{17,25},{25,1},{2,10},{10... | collective-permute-start | bytes 1204232 | tf_op jit(solution)/shard_map/ppermute | solution.py:53
  14.6 13.9 %collective-permute-start.2 = (bf16[448,128]{1,0:T(8,128)(2,1)}, bf16[448,128]{1,0:T(8,128)(2,1)S(1)}, u32[]{:S(2)}, u32[]{:S(2)}) collective-permute-start(bf16[448,128]{1,0:T(8,128)(2,1)} %bitcast.31), channel_id=1, source_target_pairs={{0,4},{1,36},{2,68},{3,100},{4,0},{5,32},{6,64},{7,96},{32,5},{33,... | collective-permute-start | bytes 344072 | tf_op jit(solution)/shard_map/ppermute | solution.py:110
  23.4 10.2 %collective-permute-start.3 = (bf16[448,128]{1,0:T(8,128)(2,1)}, bf16[448,128]{1,0:T(8,128)(2,1)S(1)}, u32[]{:S(2)}, u32[]{:S(2)}) collective-permute-start(bf16[448,128]{1,0:T(8,128)(2,1)} %bitcast.32), channel_id=1, source_target_pairs={{0,6},{1,38},{2,70},{3,102},{4,2},{5,34},{6,66},{7,98},{32,7},{33,... | collective-permute-start | bytes 344072 | tf_op jit(solution)/shard_map/ppermute | solution.py:110
  28.5 6.0 %collective-permute-start.4 = (bf16[448,128]{1,0:T(8,128)(2,1)S(1)}, bf16[448,128]{1,0:T(8,128)(2,1)S(1)}, u32[]{:S(2)}, u32[]{:S(2)}) collective-permute-start(bf16[448,128]{1,0:T(8,128)(2,1)S(1)} %collective-permute-done.refs_0_), channel_id=1, source_target_pairs={{0,1},{1,0},{2,3},{3,2},{4,5},{5,4},{6,7},{7,6},{8,9},{9,8},{10,11... | collective-permute-start | bytes 344072 | tf_op jit(solution)/shard_map/ppermute | solution.py:57
  33.6 1.8 collective-permute-start.5
  34.5 1.4 collective-permute-start.6
  35.5 1.3 collective-permute-start.7
  35.9 23.5 %copy-start.18 = (s32[128,2]{0,1:T(2,128)S(1)}, s32[128,2]{0,1:T(2,128)}, u32[]{:S(2)}) copy-start(s32[128,2]{0,1:T(2,128)} %param.16) | copy-start | bytes 3076
  35.9 23.5 %copy-start.17 = (s32[128,2]{0,1:T(2,128)S(1)}, s32[128,2]{0,1:T(2,128)}, u32[]{:S(2)}) copy-start(s32[128,2]{0,1:T(2,128)} %param.17) | copy-start | bytes 3076
  38.8 8.6 %collective-permute-start.12 = (bf16[128,896]{1,0:T(8,128)(2,1)S(1)}, bf16[128,896]{1,0:T(8,128)(2,1)S(1)}, u32[]{:S(2)}, u32[]{:S(2)}) collective-permute-start(bf16[128,896]{1,0:T(8,128)(2,1)S(1)} %get-tuple-element.40), channel_id=1, source_target_pairs={{0,32},{32,64},{64,96},{96,0},{1,33},{33,65},{65,97},{97,1},{2,34}... | collective-permute-start | bytes 688136 | tf_op jit(solution)/shard_map/ppermute | solution.py:53
  38.9 12.5 %collective-permute-start.13 = (bf16[128,896]{1,0:T(8,128)(2,1)S(1)}, bf16[128,896]{1,0:T(8,128)(2,1)S(1)}, u32[]{:S(2)}, u32[]{:S(2)}) collective-permute-start(bf16[128,896]{1,0:T(8,128)(2,1)S(1)} %get-tuple-element.41), channel_id=1, source_target_pairs={{0,64},{32,96},{64,0},{96,32},{1,65},{33,97},{65,1},{97,33},{2,66}... | collective-permute-start | bytes 688136 | tf_op jit(solution)/shard_map/ppermute | solution.py:53
  41.2 11.0 %collective-permute-start.14 = (bf16[128,896]{1,0:T(8,128)(2,1)S(1)}, bf16[128,896]{1,0:T(8,128)(2,1)S(1)}, u32[]{:S(2)}, u32[]{:S(2)}) collective-permute-start(bf16[128,896]{1,0:T(8,128)(2,1)S(1)} %get-tuple-element.42), channel_id=1, source_target_pairs={{0,96},{32,0},{64,32},{96,64},{1,97},{33,1},{65,33},{97,65},{2,98}... | collective-permute-start | bytes 688136 | tf_op jit(solution)/shard_map/ppermute | solution.py:53
  53.1 16.1 %collective-permute-start.15 = (bf16[136,896]{1,0:T(8,128)(2,1)S(1)}, bf16[136,896]{1,0:T(8,128)(2,1)S(1)}, u32[]{:S(2)}, u32[]{:S(2)}) collective-permute-start(bf16[136,896]{1,0:T(8,128)(2,1)S(1)} %pad_maximum_fusion.refs_0_), channel_id=1, source_target_pairs={{0,2},{2,4},{4,6},{6,0},{1,3},{3,5},{5,7},{7,1},{8,10},{10,12},{12... | collective-permute-start | bytes 731144 | tf_op jit(solution)/shard_map/ppermute | solution.py:53
  53.2 20.5 %collective-permute-start.16 = (bf16[136,896]{1,0:T(8,128)(2,1)S(1)}, bf16[136,896]{1,0:T(8,128)(2,1)S(1)}, u32[]{:S(2)}, u32[]{:S(2)}) collective-permute-start(bf16[136,896]{1,0:T(8,128)(2,1)S(1)} %pad_maximum_fusion.refs_0_), channel_id=1, source_target_pairs={{0,4},{2,6},{4,0},{6,2},{1,5},{3,7},{5,1},{7,3},{8,12},{10,14},{12... | collective-permute-start | bytes 731144 | tf_op jit(solution)/shard_map/ppermute | solution.py:53
  59.5 22.7 %collective-permute-start.17 = (bf16[136,896]{1,0:T(8,128)(2,1)S(1)}, bf16[136,896]{1,0:T(8,128)(2,1)S(1)}, u32[]{:S(2)}, u32[]{:S(2)}) collective-permute-start(bf16[136,896]{1,0:T(8,128)(2,1)S(1)} %pad_maximum_fusion.refs_0_), channel_id=1, source_target_pairs={{0,6},{2,0},{4,2},{6,4},{1,7},{3,1},{5,3},{7,5},{8,14},{10,8},{12,... | collective-permute-start | bytes 731144 | tf_op jit(solution)/shard_map/ppermute | solution.py:53
  59.5 24.7 %collective-permute-start.18 = (bf16[136,896]{1,0:T(8,128)(2,1)S(1)}, bf16[136,896]{1,0:T(8,128)(2,1)S(1)}, u32[]{:S(2)}, u32[]{:S(2)}) collective-permute-start(bf16[136,896]{1,0:T(8,128)(2,1)S(1)} %pad_maximum_fusion.refs_0_), channel_id=1, source_target_pairs={{0,1},{1,0},{2,3},{3,2},{4,5},{5,4},{6,7},{7,6},{8,9},{9,8},{10,11... | collective-permute-start | bytes 731144 | tf_op jit(solution)/shard_map/ppermute | solution.py:57
  69.2 14.9 %collective-permute-start.19 = (bf16[136,896]{1,0:T(8,128)(2,1)S(1)}, bf16[136,896]{1,0:T(8,128)(2,1)S(1)}, u32[]{:S(2)}, u32[]{:S(2)}) collective-permute-start(bf16[136,896]{1,0:T(8,128)(2,1)S(1)} %collective-permute-done.15.refs_1_), channel_id=1, source_target_pairs={{0,1},{1,0},{2,3},{3,2},{4,5},{5,4},{6,7},{7,6},{8,9},{9,8},{10,11... | collective-permute-start | bytes 731144 | tf_op jit(solution)/shard_map/ppermute | solution.py:57
  73.7 10.5 %collective-permute-start.20 = (bf16[136,896]{1,0:T(8,128)(2,1)S(1)}, bf16[136,896]{1,0:T(8,128)(2,1)S(1)}, u32[]{:S(2)}, u32[]{:S(2)}) collective-permute-start(bf16[136,896]{1,0:T(8,128)(2,1)S(1)} %collective-permute-done.16.refs_2_), channel_id=1, source_target_pairs={{0,1},{1,0},{2,3},{3,2},{4,5},{5,4},{6,7},{7,6},{8,9},{9,8},{10,11... | collective-permute-start | bytes 731144 | tf_op jit(solution)/shard_map/ppermute | solution.py:57
  82.1 2.4 collective-permute-start.21
  89.1 34.6 %all-to-all-start.2 = ((bf16[32,5,8,896]{3,2,1,0:T(8,128)(2,1)}), bf16[32,5,8,896]{3,2,1,0:T(8,128)(2,1)S(1)}, u32[]{:S(2)}, u32[]{:S(2)}) async-start(bf16[32,5,8,896]{3,2,1,0:T(8,128)(2,1)} %get-tuple-element.58), calls=%async_computation.2 | async-start | bytes 4587520 | tf_op jit(solution)/shard_map/all_to_all | solution.py:377
  94.9 7.1 %collective-permute-start.22 = (bf16[7168,256]{1,0:T(8,128)(2,1)}, bf16[7168,256]{1,0:T(8,128)(2,1)S(1)}, u32[]{:S(2)}, u32[]{:S(2)}) collective-permute-start(bf16[7168,256]{1,0:T(8,128)(2,1)} %bitcast.19), channel_id=1, source_target_pairs={{0,1},{1,0},{2,3},{3,2},{4,5},{5,4},{6,7},{7,6},{8,9},{9,8},{10,11... | collective-permute-start | bytes 11010056 | tf_op jit(solution)/shard_map/ppermute | solution.py:57
  95.6 16.7 %collective-permute-start.23 = (bf16[7168,256]{1,0:T(8,128)(2,1)}, bf16[7168,256]{1,0:T(8,128)(2,1)S(1)}, u32[]{:S(2)}, u32[]{:S(2)}) collective-permute-start(bf16[7168,256]{1,0:T(8,128)(2,1)} %bitcast.22), channel_id=1, source_target_pairs={{0,1},{1,0},{2,3},{3,2},{4,5},{5,4},{6,7},{7,6},{8,9},{9,8},{10,11... | collective-permute-start | bytes 11010056 | tf_op jit(solution)/shard_map/ppermute | solution.py:57
  95.7 18.5 %collective-permute-start.24 = (bf16[256,7168]{1,0:T(8,128)(2,1)}, bf16[256,7168]{1,0:T(8,128)(2,1)}, u32[]{:S(2)}, u32[]{:S(2)}) collective-permute-start(bf16[256,7168]{1,0:T(8,128)(2,1)} %bitcast.25), channel_id=1, source_target_pairs={{0,1},{1,0},{2,3},{3,2},{4,5},{5,4},{6,7},{7,6},{8,9},{9,8},{10,11... | collective-permute-start | bytes 11010056 | tf_op jit(solution)/shard_map/ppermute | solution.py:57
  123.7 35.4 %all-to-all-start = ((bf16[32,5,8,896]{3,2,1,0:T(8,128)(2,1)}), bf16[32,5,8,896]{3,2,1,0:T(8,128)(2,1)}, u32[]{:S(2)}, u32[]{:S(2)}) async-start(bf16[32,5,8,896]{3,2,1,0:T(8,128)(2,1)} %shard_map.102), calls=%async_computation | async-start | bytes 4587520 | tf_op jit(solution)/shard_map/all_to_all | solution.py:377
  130.9 2.0 copy-start
  132.9 2.0 copy-start.2
  135.0 2.0 copy-start.4
  137.0 2.0 copy-start.7
  139.0 2.0 copy-start.10
  159.1 36.1 %all-to-all-start.3 = ((bf16[32,5,8,896]{3,2,1,0:T(8,128)(2,1)}), bf16[32,5,8,896]{3,2,1,0:T(8,128)(2,1)S(1)}, u32[]{:S(2)}, u32[]{:S(2)}) async-start(bf16[32,5,8,896]{3,2,1,0:T(8,128)(2,1)} %shard_map.105), calls=%async_computation.3 | async-start | bytes 4587520 | tf_op jit(solution)/shard_map/all_to_all | solution.py:379
  166.5 2.0 copy-start.1
  168.6 2.0 copy-start.3
  170.6 2.0 copy-start.5
  188.6 13.9 %copy-start.16 = (f32[128,2]{0,1:T(2,128)S(1)}, f32[128,2]{0,1:T(2,128)}, u32[]{:S(2)}) copy-start(f32[128,2]{0,1:T(2,128)} %param.18) | copy-start | bytes 3076
  195.2 36.0 %all-to-all-start.1 = ((bf16[32,5,8,896]{3,2,1,0:T(8,128)(2,1)}), bf16[32,5,8,896]{3,2,1,0:T(8,128)(2,1)}, u32[]{:S(2)}, u32[]{:S(2)}) async-start(bf16[32,5,8,896]{3,2,1,0:T(8,128)(2,1)} %shard_map.103), calls=%async_computation.1 | async-start | bytes 4587520 | tf_op jit(solution)/shard_map/all_to_all | solution.py:379
  206.8 32.3 %collective-permute-start.26 = (bf16[4,128,896]{2,1,0:T(8,128)(2,1)}, bf16[4,128,896]{2,1,0:T(8,128)(2,1)}, u32[]{:S(2)}, u32[]{:S(2)}) collective-permute-start(bf16[4,128,896]{2,1,0:T(8,128)(2,1)} %get-tuple-element.60), channel_id=1, source_target_pairs={{0,1},{1,0},{2,3},{3,2},{4,5},{5,4},{6,7},{7,6},{8,9},{9,8},{10,11... | collective-permute-start | bytes 2752520 | tf_op jit(solution)/shard_map/ppermute | solution.py:57
  235.5 5.8 %collective-permute-start.25 = (bf16[4,128,896]{2,1,0:T(8,128)(2,1)S(1)}, bf16[4,128,896]{2,1,0:T(8,128)(2,1)}, u32[]{:S(2)}, u32[]{:S(2)}) collective-permute-start(bf16[4,128,896]{2,1,0:T(8,128)(2,1)S(1)} %get-tuple-element.57), channel_id=1, source_target_pairs={{0,1},{1,0},{2,3},{3,2},{4,5},{5,4},{6,7},{7,6},{8,9},{9,8},{10,11... | collective-permute-start | bytes 2752520 | tf_op jit(solution)/shard_map/ppermute | solution.py:57
  241.3 28.4 %copy-start.13 = (f32[128,896]{1,0:T(8,128)S(1)}, f32[128,896]{1,0:T(8,128)}, u32[]{:S(2)}) copy-start(f32[128,896]{1,0:T(8,128)} %get-tuple-element.44) | copy-start | bytes 1376260
  243.0 11.6 %collective-permute-start.27 = (bf16[128,896]{1,0:T(8,128)(2,1)S(1)}, bf16[128,896]{1,0:T(8,128)(2,1)S(1)}, u32[]{:S(2)}, u32[]{:S(2)}) collective-permute-start(bf16[128,896]{1,0:T(8,128)(2,1)S(1)} %get-tuple-element.65), channel_id=1, source_target_pairs={{0,2},{2,4},{4,6},{6,0},{1,3},{3,5},{5,7},{7,1},{8,10},{10,12},{12... | collective-permute-start | bytes 688136 | tf_op jit(solution)/shard_map/ppermute | solution.py:53
  244.1 18.4 %collective-permute-start.28 = (bf16[128,896]{1,0:T(8,128)(2,1)S(1)}, bf16[128,896]{1,0:T(8,128)(2,1)S(1)}, u32[]{:S(2)}, u32[]{:S(2)}) collective-permute-start(bf16[128,896]{1,0:T(8,128)(2,1)S(1)} %get-tuple-element.67), channel_id=1, source_target_pairs={{0,4},{2,6},{4,0},{6,2},{1,5},{3,7},{5,1},{7,3},{8,12},{10,14},{12... | collective-permute-start | bytes 688136 | tf_op jit(solution)/shard_map/ppermute | solution.py:53
  246.6 23.2 %collective-permute-start.29 = (bf16[128,896]{1,0:T(8,128)(2,1)S(1)}, bf16[128,896]{1,0:T(8,128)(2,1)S(1)}, u32[]{:S(2)}, u32[]{:S(2)}) collective-permute-start(bf16[128,896]{1,0:T(8,128)(2,1)S(1)} %get-tuple-element.66), channel_id=1, source_target_pairs={{0,6},{2,0},{4,2},{6,4},{1,7},{3,1},{5,3},{7,5},{8,14},{10,8},{12,... | collective-permute-start | bytes 688136 | tf_op jit(solution)/shard_map/ppermute | solution.py:53
  (5 other events, 9.2 us)

commit v2 on v1

--- a/solution.py
+++ b/solution.py
@@ -219,7 +219,7 @@
     parts += [swap(value, "core") for value in parts]
     normed, one = call(
         first_kernel,
-        (pltpu.HBM((N_MP, TOK, SHARD), BF16), SLAB_SHAPE),
+        (jax.ShapeDtypeStruct((N_MP, TOK, SHARD), BF16), SLAB_SHAPE),
         2_000_000_000,
         6_000_000,
         grid=(1,),

time: 272 us -> 273 us (level)
    unnamed x40 -> x42, local copies, waits for them, and re-layouts: 26.6 us -> 27.9 us
where the time goes in v2:
time: 273 us; the launch traced here: 272 us
  waiting for transfers between devices  111 us (41%)
  starting transfers between devices  85.8 us (31%)
  Pallas kernels  40.7 us (15%)
  local copies, waits for them, and re-layouts  28.8 us (11%)
  other arithmetic  4.79 us (2%)
    ppermute x12, waiting for transfers between devices, shift(): lax.ppermute(value, axis, [(i, (i + step) % size) for i in range(size)])  41.9 us
    all_to_all x2, waiting for transfers between devices, shards(): lax.all_to_all(half_out, EXPERT, split_axis=0, concat_axis=0, tiled=True)  29.8 us
    unnamed x42, local copies, waits for them, and re-layouts  27.9 us
    pallas_call x2, Pallas kernels, experts(): call(experts_kernel, SLAB_SHAPE, 2 * SLOTS * D * HID * 6, 27000000, 34, g...  22.9 us
    ppermute x14, starting transfers between devices, swap(): return lax.ppermute(value, axis, [(0, 1), (1, 0)])  22.3 us
    ppermute x12, starting transfers between devices, shift(): lax.ppermute(value, axis, [(i, (i + step) % size) for i in range(size)])  20 us
    all_to_all x2, waiting for transfers between devices, shards(): lax.all_to_all(rows, EXPERT, split_axis=0, concat_axis=0, tiled=True)  16.4 us
    ppermute x4, starting transfers between devices, project(): features.append(lax.ppermute(flipped, ('y',) + MP, pairs))  15.7 us
  transfers between devices with their start and end apart: 34, of which 21 were waited for; matrix products, arithmetic and copies ran while one was open for 1% of the time, Pallas kernels for 13%

profile of v2, /device:TPU:1, one launch (start us, length us, event | category | flops | bytes accessed | tf_op | source)
XLA Modules:
  0.0 271.8 jit_solution(3562323095860168715)
XLA Ops:
  0.0 2.5 collective-permute-start.8
  2.5 4.0 %collective-permute-start = (bf16[448,128]{1,0:T(8,128)(2,1)}, bf16[448,128]{1,0:T(8,128)(2,1)S(1)}, u32[]{:S(2)}, u32[]{:S(2)}) collective-permute-start(bf16[448,128]{1,0:T(8,128)(2,1)} %bitcast.29), channel_id=1, source_target_pairs={{0,0},{1,32},{2,64},{3,96},{4,4},{5,36},{6,68},{7,100},{32,1},{33,... | collective-permute-start | bytes 344072 | tf_op jit(solution)/shard_map/ppermute | solution.py:110
  6.5 2.8 %collective-permute-start.1 = (bf16[448,128]{1,0:T(8,128)(2,1)}, bf16[448,128]{1,0:T(8,128)(2,1)S(1)}, u32[]{:S(2)}, u32[]{:S(2)}) collective-permute-start(bf16[448,128]{1,0:T(8,128)(2,1)} %bitcast.30), channel_id=1, source_target_pairs={{0,2},{1,34},{2,66},{3,98},{4,6},{5,38},{6,70},{7,102},{32,3},{33,... | collective-permute-start | bytes 344072 | tf_op jit(solution)/shard_map/ppermute | solution.py:110
  10.3 2.8 %collective-permute-start.10 = (bf16[224,896]{1,0:T(8,128)(2,1)S(1)}, bf16[224,896]{1,0:T(8,128)(2,1)S(1)}, u32[]{:S(2)}, u32[]{:S(2)}) collective-permute-start(bf16[224,896]{1,0:T(8,128)(2,1)S(1)} %constant_dynamic-update-slice_fusion.refs_8_), channel_id=1, source_target_pairs={{0,16},{8,24},{16,0},{24,8},{1,17},{9,25},{17,1},{25,9},{2,18},{10... | collective-permute-start | bytes 1204232 | tf_op jit(solution)/shard_map/ppermute | solution.py:53
  14.6 8.8 %collective-permute-start.2 = (bf16[448,128]{1,0:T(8,128)(2,1)}, bf16[448,128]{1,0:T(8,128)(2,1)S(1)}, u32[]{:S(2)}, u32[]{:S(2)}) collective-permute-start(bf16[448,128]{1,0:T(8,128)(2,1)} %bitcast.31), channel_id=1, source_target_pairs={{0,4},{1,36},{2,68},{3,100},{4,0},{5,32},{6,64},{7,96},{32,5},{33,... | collective-permute-start | bytes 344072 | tf_op jit(solution)/shard_map/ppermute | solution.py:110
  23.4 5.1 %collective-permute-done.2.refs_2_ = bf16[448,128]{1,0:T(8,128)(2,1)S(1)} collective-permute-done((bf16[448,128]{1,0:T(8,128)(2,1)}, bf16[448,128]{1,0:T(8,128)(2,1)S(1)}, u32[]{:S(2)}, u32[]{:S(2)}) %collective-permute-start.2) | collective-permute-done | bytes 114720 | tf_op jit(solution)/shard_map/ppermute | solution.py:110
  28.5 5.1 %collective-permute-done.3.refs_3_ = bf16[448,128]{1,0:T(8,128)(2,1)S(1)} collective-permute-done((bf16[448,128]{1,0:T(8,128)(2,1)}, bf16[448,128]{1,0:T(8,128)(2,1)S(1)}, u32[]{:S(2)}, u32[]{:S(2)}) %collective-permute-start.3) | collective-permute-done | bytes 114720 | tf_op jit(solution)/shard_map/ppermute | solution.py:110
  36.8 2.0 shard_map.100
  38.9 2.2 collective-permute-start.13
  42.3 5.1 %collective-permute-done.12 = bf16[128,896]{1,0:T(8,128)(2,1)S(1)} collective-permute-done((bf16[128,896]{1,0:T(8,128)(2,1)S(1)}, bf16[128,896]{1,0:T(8,128)(2,1)S(1)}, u32[]{:S(2)}, u32[]{:S(2)}) %collective-permute-start.12) | collective-permute-done | bytes 229408 | tf_op jit(solution)/shard_map/ppermute | solution.py:53
  47.4 4.1 %collective-permute-done.13 = bf16[128,896]{1,0:T(8,128)(2,1)S(1)} collective-permute-done((bf16[128,896]{1,0:T(8,128)(2,1)S(1)}, bf16[128,896]{1,0:T(8,128)(2,1)S(1)}, u32[]{:S(2)}, u32[]{:S(2)}) %collective-permute-start.13) | collective-permute-done | bytes 229408 | tf_op jit(solution)/shard_map/ppermute | solution.py:53
  53.2 6.3 %collective-permute-start.16 = (bf16[136,896]{1,0:T(8,128)(2,1)S(1)}, bf16[136,896]{1,0:T(8,128)(2,1)S(1)}, u32[]{:S(2)}, u32[]{:S(2)}) collective-permute-start(bf16[136,896]{1,0:T(8,128)(2,1)S(1)} %pad_maximum_fusion.refs_0_), channel_id=1, source_target_pairs={{0,4},{2,6},{4,0},{6,2},{1,5},{3,7},{5,1},{7,3},{8,12},{10,14},{12... | collective-permute-start | bytes 731144 | tf_op jit(solution)/shard_map/ppermute | solution.py:53
  59.5 2.2 collective-permute-start.18
  61.7 7.6 %collective-permute-done.15.refs_1_ = bf16[136,896]{1,0:T(8,128)(2,1)S(1)} collective-permute-done((bf16[136,896]{1,0:T(8,128)(2,1)S(1)}, bf16[136,896]{1,0:T(8,128)(2,1)S(1)}, u32[]{:S(2)}, u32[]{:S(2)}) %collective-permute-start.15) | collective-permute-done | bytes 243744 | tf_op jit(solution)/shard_map/ppermute | solution.py:53
  70.1 3.6 %collective-permute-done.16.refs_2_ = bf16[136,896]{1,0:T(8,128)(2,1)S(1)} collective-permute-done((bf16[136,896]{1,0:T(8,128)(2,1)S(1)}, bf16[136,896]{1,0:T(8,128)(2,1)S(1)}, u32[]{:S(2)}, u32[]{:S(2)}) %collective-permute-start.16) | collective-permute-done | bytes 243744 | tf_op jit(solution)/shard_map/ppermute | solution.py:53
  73.7 8.4 %collective-permute-start.20 = (bf16[136,896]{1,0:T(8,128)(2,1)S(1)}, bf16[136,896]{1,0:T(8,128)(2,1)S(1)}, u32[]{:S(2)}, u32[]{:S(2)}) collective-permute-start(bf16[136,896]{1,0:T(8,128)(2,1)S(1)} %collective-permute-done.16.refs_2_), channel_id=1, source_target_pairs={{0,1},{1,0},{2,3},{3,2},{4,5},{5,4},{6,7},{7,6},{8,9},{9,8},{10,11... | collective-permute-start | bytes 731144 | tf_op jit(solution)/shard_map/ppermute | solution.py:57
  84.5 4.5 %shard_map.101 = (bf16[8,128,896]{2,1,0:T(8,128)(2,1)S(1)}, bf16[32,5,8,896]{3,2,1,0:T(8,128)(2,1)}) custom-call(s32[5]{0:T(128)S(1)} %stack.39.place, s32[2,128]{1,0:T(2,128)S(1)} %copy.30.codes, bf16[136,896]{1,0:T(8,128)(2,1)S(1)} %pad_maximum_fusion.refs_0_, bf16[136,896]{1,0:T(8,128)(2,1)S(1)} %collective-permute-done.15.refs_1_, ...), custom_call_target="tpu_custom_call" | custom-call | flops 2000000000 | bytes 6000000 | tf_op jit(solution)/shard_map/pallas_call | solution.py:220
  90.3 5.8 %all-to-all-start.2 = ((bf16[32,5,8,896]{3,2,1,0:T(8,128)(2,1)}), bf16[32,5,8,896]{3,2,1,0:T(8,128)(2,1)S(1)}, u32[]{:S(2)}, u32[]{:S(2)}) async-start(bf16[32,5,8,896]{3,2,1,0:T(8,128)(2,1)} %get-tuple-element.58), calls=%async_computation.2 | async-start | bytes 4587520 | tf_op jit(solution)/shard_map/all_to_all | solution.py:377
  98.9 2.8 %shard_map.102 = bf16[32,5,8,896]{3,2,1,0:T(8,128)(2,1)} custom-call(s32[2,128]{1,0:T(2,128)S(1)} %copy.30.codes, bf16[8,128,896]{2,1,0:T(8,128)(2,1)S(1)} %copy-done.13), custom_call_target="tpu_custom_call" | custom-call | flops 1000000000 | bytes 4000000 | tf_op jit(solution)/shard_map/pallas_call | solution.py:230
  105.1 8.6 %collective-permute-done.23.up_b = bf16[7168,256]{1,0:T(8,128)(2,1)S(1)} collective-permute-done((bf16[7168,256]{1,0:T(8,128)(2,1)}, bf16[7168,256]{1,0:T(8,128)(2,1)S(1)}, u32[]{:S(2)}, u32[]{:S(2)}) %collective-permute-start.23) | collective-permute-done | bytes 3670048 | tf_op jit(solution)/shard_map/ppermute | solution.py:57
  113.6 1.8 copy-done.9
  115.5 9.4 %all-to-all-done.2.units = bf16[32,5,8,896]{3,2,1,0:T(8,128)(2,1)S(1)} async-done(((bf16[32,5,8,896]{3,2,1,0:T(8,128)(2,1)}), bf16[32,5,8,896]{3,2,1,0:T(8,128)(2,1)S(1)}, u32[]{:S(2)}, u32[]{:S(2)}) %all-to-all-start.2) | async-done | bytes 2293792 | tf_op jit(solution)/shard_map/all_to_all | solution.py:377
  124.9 7.2 %all-to-all-start = ((bf16[32,5,8,896]{3,2,1,0:T(8,128)(2,1)}), bf16[32,5,8,896]{3,2,1,0:T(8,128)(2,1)}, u32[]{:S(2)}, u32[]{:S(2)}) async-start(bf16[32,5,8,896]{3,2,1,0:T(8,128)(2,1)} %shard_map.102), calls=%async_computation | async-start | bytes 4587520 | tf_op jit(solution)/shard_map/all_to_all | solution.py:377
  132.2 2.0 copy-done
  134.2 2.0 copy-done.2
  136.2 2.0 copy-done.4
  138.3 2.0 copy-done.7
  140.3 2.0 copy-done.10
  142.3 11.0 %shard_map.105 = bf16[32,5,8,896]{3,2,1,0:T(8,128)(2,1)} custom-call(bf16[32,5,8,896]{3,2,1,0:T(8,128)(2,1)S(1)} %all-to-all-done.2.units, bf16[7168,256]{1,0:T(8,128)(2,1)S(1)} %bitcast.20, bf16[7168,256]{1,0:T(8,128)(2,1)S(1)} %bitcast.23, bf16[7168,256]{1,0:T(8,128)(2,1)S(1)} %copy-done.7, bf16[7168,256]{1,0:T(8,128)(2,1)S(1)} %copy-done.10, ...), custom_call_target="tpu_custom_call" | custom-call | flops 3523215360 | bytes 27000000 | tf_op jit(solution)/shard_map/pallas_call | solution.py:279
  153.4 7.0 %all-to-all-done.units = bf16[32,5,8,896]{3,2,1,0:T(8,128)(2,1)} async-done(((bf16[32,5,8,896]{3,2,1,0:T(8,128)(2,1)}), bf16[32,5,8,896]{3,2,1,0:T(8,128)(2,1)}, u32[]{:S(2)}, u32[]{:S(2)}) %all-to-all-start) | async-done | bytes 2293792 | tf_op jit(solution)/shard_map/all_to_all | solution.py:377
  160.3 7.4 %all-to-all-start.3 = ((bf16[32,5,8,896]{3,2,1,0:T(8,128)(2,1)}), bf16[32,5,8,896]{3,2,1,0:T(8,128)(2,1)S(1)}, u32[]{:S(2)}, u32[]{:S(2)}) async-start(bf16[32,5,8,896]{3,2,1,0:T(8,128)(2,1)} %shard_map.105), calls=%async_computation.3 | async-start | bytes 4587520 | tf_op jit(solution)/shard_map/all_to_all | solution.py:379
  167.8 2.0 copy-done.1
  169.8 2.0 copy-done.3
  171.9 2.0 copy-done.5
  173.9 2.0 copy-done.8
  176.0 2.0 copy-done.11
  178.0 11.9 %shard_map.103 = bf16[32,5,8,896]{3,2,1,0:T(8,128)(2,1)} custom-call(bf16[32,5,8,896]{3,2,1,0:T(8,128)(2,1)} %all-to-all-done.units, bf16[7168,256]{1,0:T(8,128)(2,1)S(1)} %bitcast.21, bf16[7168,256]{1,0:T(8,128)(2,1)S(1)} %bitcast.24, bf16[7168,256]{1,0:T(8,128)(2,1)S(1)} %copy-done.8, bf16[7168,256]{1,0:T(8,128)(2,1)S(1)} %copy-done.11, ...), custom_call_target="tpu_custom_call" | custom-call | flops 3523215360 | bytes 27000000 | tf_op jit(solution)/shard_map/pallas_call | solution.py:279
  189.8 6.6 %all-to-all-done.3.units = bf16[32,5,8,896]{3,2,1,0:T(8,128)(2,1)S(1)} async-done(((bf16[32,5,8,896]{3,2,1,0:T(8,128)(2,1)}), bf16[32,5,8,896]{3,2,1,0:T(8,128)(2,1)S(1)}, u32[]{:S(2)}, u32[]{:S(2)}) %all-to-all-start.3) | async-done | bytes 2293792 | tf_op jit(solution)/shard_map/all_to_all | solution.py:379
  196.4 7.3 %all-to-all-start.1 = ((bf16[32,5,8,896]{3,2,1,0:T(8,128)(2,1)}), bf16[32,5,8,896]{3,2,1,0:T(8,128)(2,1)}, u32[]{:S(2)}, u32[]{:S(2)}) async-start(bf16[32,5,8,896]{3,2,1,0:T(8,128)(2,1)} %shard_map.103), calls=%async_computation.1 | async-start | bytes 4587520 | tf_op jit(solution)/shard_map/all_to_all | solution.py:379
  203.9 4.1 %shard_map.106 = (bf16[4,128,896]{2,1,0:T(8,128)(2,1)S(1)}, bf16[4,128,896]{2,1,0:T(8,128)(2,1)}) custom-call(s32[5]{0:T(128)S(1)} %stack.39.place, s32[128,2]{1,0:T(8,128)S(1)} %add_select_fusion.codes, f32[128,2]{1,0:T(8,128)S(1)} %copy.32.probs, bf16[32,5,8,896]{3,2,1,0:T(8,128)(2,1)S(1)} %all-to-all-done.3.units), custom_call_target="tpu_custom_call" | custom-call | flops 2500000000 | bytes 6000000 | tf_op jit(solution)/shard_map/pallas_call | solution.py:327
  209.1 23.3 %all-to-all-done.1.units = bf16[32,5,8,896]{3,2,1,0:T(8,128)(2,1)} async-done(((bf16[32,5,8,896]{3,2,1,0:T(8,128)(2,1)}), bf16[32,5,8,896]{3,2,1,0:T(8,128)(2,1)}, u32[]{:S(2)}, u32[]{:S(2)}) %all-to-all-start.1) | async-done | bytes 2293792 | tf_op jit(solution)/shard_map/all_to_all | solution.py:379
  232.4 4.3 %shard_map.104 = (bf16[4,128,896]{2,1,0:T(8,128)(2,1)S(1)}, bf16[4,128,896]{2,1,0:T(8,128)(2,1)S(1)}) custom-call(s32[5]{0:T(128)S(1)} %stack.39.place, s32[128,2]{1,0:T(8,128)S(1)} %add_select_fusion.codes, f32[128,2]{1,0:T(8,128)S(1)} %copy.32.probs, bf16[32,5,8,896]{3,2,1,0:T(8,128)(2,1)} %all-to-all-done.1.units), custom_call_target="tpu_custom_call" | custom-call | flops 2500000000 | bytes 6000000 | tf_op jit(solution)/shard_map/pallas_call | solution.py:327
  236.7 3.6 %collective-permute-start.25 = (bf16[4,128,896]{2,1,0:T(8,128)(2,1)S(1)}, bf16[4,128,896]{2,1,0:T(8,128)(2,1)}, u32[]{:S(2)}, u32[]{:S(2)}) collective-permute-start(bf16[4,128,896]{2,1,0:T(8,128)(2,1)S(1)} %get-tuple-element.57), channel_id=1, source_target_pairs={{0,1},{1,0},{2,3},{3,2},{4,5},{5,4},{6,7},{7,6},{8,9},{9,8},{10,11... | collective-permute-start | bytes 2752520 | tf_op jit(solution)/shard_map/ppermute | solution.py:57
  245.4 2.5 collective-permute-start.28
  247.8 2.3 collective-permute-start.29
  250.2 5.6 %collective-permute-done.27 = bf16[128,896]{1,0:T(8,128)(2,1)S(1)} collective-permute-done((bf16[128,896]{1,0:T(8,128)(2,1)S(1)}, bf16[128,896]{1,0:T(8,128)(2,1)S(1)}, u32[]{:S(2)}, u32[]{:S(2)}) %collective-permute-start.27) | collective-permute-done | bytes 229408 | tf_op jit(solution)/shard_map/ppermute | solution.py:53
  255.8 7.9 %collective-permute-done.28 = bf16[128,896]{1,0:T(8,128)(2,1)S(1)} collective-permute-done((bf16[128,896]{1,0:T(8,128)(2,1)S(1)}, bf16[128,896]{1,0:T(8,128)(2,1)S(1)}, u32[]{:S(2)}, u32[]{:S(2)}) %collective-permute-start.28) | collective-permute-done | bytes 229408 | tf_op jit(solution)/shard_map/ppermute | solution.py:53
  263.7 7.2 %collective-permute-done.29 = bf16[128,896]{1,0:T(8,128)(2,1)S(1)} collective-permute-done((bf16[128,896]{1,0:T(8,128)(2,1)S(1)}, bf16[128,896]{1,0:T(8,128)(2,1)S(1)}, u32[]{:S(2)}, u32[]{:S(2)}) %collective-permute-start.29) | collective-permute-done | bytes 229408 | tf_op jit(solution)/shard_map/ppermute | solution.py:53
  (92 shorter events, 26.3 us)
Async XLA Ops:
  0.0 42.2 %copy-start.16 = (f32[896]{0:T(1024)S(1)}, f32[896]{0:T(1024)}, u32[]{:S(2)}) copy-start(f32[896]{0:T(1024)} %param.15) | copy-start | bytes 10756
  0.0 52.2 %copy-start.15 = (bf16[128,896]{1,0:T(8,128)(2,1)S(1)}, bf16[128,896]{1,0:T(8,128)(2,1)}, u32[]{:S(2)}) copy-start(bf16[128,896]{1,0:T(8,128)(2,1)} %param.14) | copy-start | bytes 688132
  0.0 10.3 %collective-permute-start.8 = (bf16[112,896]{1,0:T(8,128)(2,1)}, bf16[112,896]{1,0:T(8,128)(2,1)S(1)}, u32[]{:S(2)}, u32[]{:S(2)}) collective-permute-start(bf16[112,896]{1,0:T(8,128)(2,1)} %param.13), channel_id=1, source_target_pairs={{0,128},{128,0},{1,129},{129,1},{2,130},{130,2},{3,131},{131,3},{4... | collective-permute-start | bytes 602120 | tf_op jit(solution)/shard_map/ppermute | solution.py:57
  2.5 12.1 %collective-permute-start = (bf16[448,128]{1,0:T(8,128)(2,1)}, bf16[448,128]{1,0:T(8,128)(2,1)S(1)}, u32[]{:S(2)}, u32[]{:S(2)}) collective-permute-start(bf16[448,128]{1,0:T(8,128)(2,1)} %bitcast.29), channel_id=1, source_target_pairs={{0,0},{1,32},{2,64},{3,96},{4,4},{5,36},{6,68},{7,100},{32,1},{33,... | collective-permute-start | bytes 344072 | tf_op jit(solution)/shard_map/ppermute | solution.py:110
  6.5 16.9 %collective-permute-start.1 = (bf16[448,128]{1,0:T(8,128)(2,1)}, bf16[448,128]{1,0:T(8,128)(2,1)S(1)}, u32[]{:S(2)}, u32[]{:S(2)}) collective-permute-start(bf16[448,128]{1,0:T(8,128)(2,1)} %bitcast.30), channel_id=1, source_target_pairs={{0,2},{1,34},{2,66},{3,98},{4,6},{5,38},{6,70},{7,102},{32,3},{33,... | collective-permute-start | bytes 344072 | tf_op jit(solution)/shard_map/ppermute | solution.py:110
  10.3 26.5 %collective-permute-start.10 = (bf16[224,896]{1,0:T(8,128)(2,1)S(1)}, bf16[224,896]{1,0:T(8,128)(2,1)S(1)}, u32[]{:S(2)}, u32[]{:S(2)}) collective-permute-start(bf16[224,896]{1,0:T(8,128)(2,1)S(1)} %constant_dynamic-update-slice_fusion.refs_8_), channel_id=1, source_target_pairs={{0,16},{8,24},{16,0},{24,8},{1,17},{9,25},{17,1},{25,9},{2,18},{10... | collective-permute-start | bytes 1204232 | tf_op jit(solution)/shard_map/ppermute | solution.py:53
  13.1 23.7 %collective-permute-start.11 = (bf16[224,896]{1,0:T(8,128)(2,1)S(1)}, bf16[224,896]{1,0:T(8,128)(2,1)S(1)}, u32[]{:S(2)}, u32[]{:S(2)}) collective-permute-start(bf16[224,896]{1,0:T(8,128)(2,1)S(1)} %constant_dynamic-update-slice_fusion.refs_8_), channel_id=1, source_target_pairs={{0,24},{8,0},{16,8},{24,16},{1,25},{9,1},{17,9},{25,17},{2,26},{10... | collective-permute-start | bytes 1204232 | tf_op jit(solution)/shard_map/ppermute | solution.py:53
  14.0 22.8 %collective-permute-start.9 = (bf16[224,896]{1,0:T(8,128)(2,1)S(1)}, bf16[224,896]{1,0:T(8,128)(2,1)S(1)}, u32[]{:S(2)}, u32[]{:S(2)}) collective-permute-start(bf16[224,896]{1,0:T(8,128)(2,1)S(1)} %constant_dynamic-update-slice_fusion.refs_8_), channel_id=1, source_target_pairs={{0,8},{8,16},{16,24},{24,0},{1,9},{9,17},{17,25},{25,1},{2,10},{10... | collective-permute-start | bytes 1204232 | tf_op jit(solution)/shard_map/ppermute | solution.py:53
  14.6 13.9 %collective-permute-start.2 = (bf16[448,128]{1,0:T(8,128)(2,1)}, bf16[448,128]{1,0:T(8,128)(2,1)S(1)}, u32[]{:S(2)}, u32[]{:S(2)}) collective-permute-start(bf16[448,128]{1,0:T(8,128)(2,1)} %bitcast.31), channel_id=1, source_target_pairs={{0,4},{1,36},{2,68},{3,100},{4,0},{5,32},{6,64},{7,96},{32,5},{33,... | collective-permute-start | bytes 344072 | tf_op jit(solution)/shard_map/ppermute | solution.py:110
  23.4 10.2 %collective-permute-start.3 = (bf16[448,128]{1,0:T(8,128)(2,1)}, bf16[448,128]{1,0:T(8,128)(2,1)S(1)}, u32[]{:S(2)}, u32[]{:S(2)}) collective-permute-start(bf16[448,128]{1,0:T(8,128)(2,1)} %bitcast.32), channel_id=1, source_target_pairs={{0,6},{1,38},{2,70},{3,102},{4,2},{5,34},{6,66},{7,98},{32,7},{33,... | collective-permute-start | bytes 344072 | tf_op jit(solution)/shard_map/ppermute | solution.py:110
  28.5 6.0 %collective-permute-start.4 = (bf16[448,128]{1,0:T(8,128)(2,1)S(1)}, bf16[448,128]{1,0:T(8,128)(2,1)S(1)}, u32[]{:S(2)}, u32[]{:S(2)}) collective-permute-start(bf16[448,128]{1,0:T(8,128)(2,1)S(1)} %collective-permute-done.refs_0_), channel_id=1, source_target_pairs={{0,1},{1,0},{2,3},{3,2},{4,5},{5,4},{6,7},{7,6},{8,9},{9,8},{10,11... | collective-permute-start | bytes 344072 | tf_op jit(solution)/shard_map/ppermute | solution.py:57
  33.6 1.8 collective-permute-start.5
  34.5 1.4 collective-permute-start.6
  35.5 1.3 collective-permute-start.7
  35.9 23.5 %copy-start.19 = (s32[128,2]{0,1:T(2,128)S(1)}, s32[128,2]{0,1:T(2,128)}, u32[]{:S(2)}) copy-start(s32[128,2]{0,1:T(2,128)} %param.16) | copy-start | bytes 3076
  35.9 23.5 %copy-start.18 = (s32[128,2]{0,1:T(2,128)S(1)}, s32[128,2]{0,1:T(2,128)}, u32[]{:S(2)}) copy-start(s32[128,2]{0,1:T(2,128)} %param.17) | copy-start | bytes 3076
  38.8 8.6 %collective-permute-start.12 = (bf16[128,896]{1,0:T(8,128)(2,1)S(1)}, bf16[128,896]{1,0:T(8,128)(2,1)S(1)}, u32[]{:S(2)}, u32[]{:S(2)}) collective-permute-start(bf16[128,896]{1,0:T(8,128)(2,1)S(1)} %get-tuple-element.40), channel_id=1, source_target_pairs={{0,32},{32,64},{64,96},{96,0},{1,33},{33,65},{65,97},{97,1},{2,34}... | collective-permute-start | bytes 688136 | tf_op jit(solution)/shard_map/ppermute | solution.py:53
  38.9 12.5 %collective-permute-start.13 = (bf16[128,896]{1,0:T(8,128)(2,1)S(1)}, bf16[128,896]{1,0:T(8,128)(2,1)S(1)}, u32[]{:S(2)}, u32[]{:S(2)}) collective-permute-start(bf16[128,896]{1,0:T(8,128)(2,1)S(1)} %get-tuple-element.41), channel_id=1, source_target_pairs={{0,64},{32,96},{64,0},{96,32},{1,65},{33,97},{65,1},{97,33},{2,66}... | collective-permute-start | bytes 688136 | tf_op jit(solution)/shard_map/ppermute | solution.py:53
  41.2 11.0 %collective-permute-start.14 = (bf16[128,896]{1,0:T(8,128)(2,1)S(1)}, bf16[128,896]{1,0:T(8,128)(2,1)S(1)}, u32[]{:S(2)}, u32[]{:S(2)}) collective-permute-start(bf16[128,896]{1,0:T(8,128)(2,1)S(1)} %get-tuple-element.42), channel_id=1, source_target_pairs={{0,96},{32,0},{64,32},{96,64},{1,97},{33,1},{65,33},{97,65},{2,98}... | collective-permute-start | bytes 688136 | tf_op jit(solution)/shard_map/ppermute | solution.py:53
  53.1 16.1 %collective-permute-start.15 = (bf16[136,896]{1,0:T(8,128)(2,1)S(1)}, bf16[136,896]{1,0:T(8,128)(2,1)S(1)}, u32[]{:S(2)}, u32[]{:S(2)}) collective-permute-start(bf16[136,896]{1,0:T(8,128)(2,1)S(1)} %pad_maximum_fusion.refs_0_), channel_id=1, source_target_pairs={{0,2},{2,4},{4,6},{6,0},{1,3},{3,5},{5,7},{7,1},{8,10},{10,12},{12... | collective-permute-start | bytes 731144 | tf_op jit(solution)/shard_map/ppermute | solution.py:53
  53.2 20.5 %collective-permute-start.16 = (bf16[136,896]{1,0:T(8,128)(2,1)S(1)}, bf16[136,896]{1,0:T(8,128)(2,1)S(1)}, u32[]{:S(2)}, u32[]{:S(2)}) collective-permute-start(bf16[136,896]{1,0:T(8,128)(2,1)S(1)} %pad_maximum_fusion.refs_0_), channel_id=1, source_target_pairs={{0,4},{2,6},{4,0},{6,2},{1,5},{3,7},{5,1},{7,3},{8,12},{10,14},{12... | collective-permute-start | bytes 731144 | tf_op jit(solution)/shard_map/ppermute | solution.py:53
  59.5 22.7 %collective-permute-start.17 = (bf16[136,896]{1,0:T(8,128)(2,1)S(1)}, bf16[136,896]{1,0:T(8,128)(2,1)S(1)}, u32[]{:S(2)}, u32[]{:S(2)}) collective-permute-start(bf16[136,896]{1,0:T(8,128)(2,1)S(1)} %pad_maximum_fusion.refs_0_), channel_id=1, source_target_pairs={{0,6},{2,0},{4,2},{6,4},{1,7},{3,1},{5,3},{7,5},{8,14},{10,8},{12,... | collective-permute-start | bytes 731144 | tf_op jit(solution)/shard_map/ppermute | solution.py:53
  59.5 24.7 %collective-permute-start.18 = (bf16[136,896]{1,0:T(8,128)(2,1)S(1)}, bf16[136,896]{1,0:T(8,128)(2,1)S(1)}, u32[]{:S(2)}, u32[]{:S(2)}) collective-permute-start(bf16[136,896]{1,0:T(8,128)(2,1)S(1)} %pad_maximum_fusion.refs_0_), channel_id=1, source_target_pairs={{0,1},{1,0},{2,3},{3,2},{4,5},{5,4},{6,7},{7,6},{8,9},{9,8},{10,11... | collective-permute-start | bytes 731144 | tf_op jit(solution)/shard_map/ppermute | solution.py:57
  69.2 14.9 %collective-permute-start.19 = (bf16[136,896]{1,0:T(8,128)(2,1)S(1)}, bf16[136,896]{1,0:T(8,128)(2,1)S(1)}, u32[]{:S(2)}, u32[]{:S(2)}) collective-permute-start(bf16[136,896]{1,0:T(8,128)(2,1)S(1)} %collective-permute-done.15.refs_1_), channel_id=1, source_target_pairs={{0,1},{1,0},{2,3},{3,2},{4,5},{5,4},{6,7},{7,6},{8,9},{9,8},{10,11... | collective-permute-start | bytes 731144 | tf_op jit(solution)/shard_map/ppermute | solution.py:57
  73.7 10.5 %collective-permute-start.20 = (bf16[136,896]{1,0:T(8,128)(2,1)S(1)}, bf16[136,896]{1,0:T(8,128)(2,1)S(1)}, u32[]{:S(2)}, u32[]{:S(2)}) collective-permute-start(bf16[136,896]{1,0:T(8,128)(2,1)S(1)} %collective-permute-done.16.refs_2_), channel_id=1, source_target_pairs={{0,1},{1,0},{2,3},{3,2},{4,5},{5,4},{6,7},{7,6},{8,9},{9,8},{10,11... | collective-permute-start | bytes 731144 | tf_op jit(solution)/shard_map/ppermute | solution.py:57
  82.1 2.4 collective-permute-start.21
  90.3 34.6 %all-to-all-start.2 = ((bf16[32,5,8,896]{3,2,1,0:T(8,128)(2,1)}), bf16[32,5,8,896]{3,2,1,0:T(8,128)(2,1)S(1)}, u32[]{:S(2)}, u32[]{:S(2)}) async-start(bf16[32,5,8,896]{3,2,1,0:T(8,128)(2,1)} %get-tuple-element.58), calls=%async_computation.2 | async-start | bytes 4587520 | tf_op jit(solution)/shard_map/all_to_all | solution.py:377
  96.1 7.1 %collective-permute-start.22 = (bf16[7168,256]{1,0:T(8,128)(2,1)}, bf16[7168,256]{1,0:T(8,128)(2,1)S(1)}, u32[]{:S(2)}, u32[]{:S(2)}) collective-permute-start(bf16[7168,256]{1,0:T(8,128)(2,1)} %bitcast.19), channel_id=1, source_target_pairs={{0,1},{1,0},{2,3},{3,2},{4,5},{5,4},{6,7},{7,6},{8,9},{9,8},{10,11... | collective-permute-start | bytes 11010056 | tf_op jit(solution)/shard_map/ppermute | solution.py:57
  96.9 16.7 %collective-permute-start.23 = (bf16[7168,256]{1,0:T(8,128)(2,1)}, bf16[7168,256]{1,0:T(8,128)(2,1)S(1)}, u32[]{:S(2)}, u32[]{:S(2)}) collective-permute-start(bf16[7168,256]{1,0:T(8,128)(2,1)} %bitcast.22), channel_id=1, source_target_pairs={{0,1},{1,0},{2,3},{3,2},{4,5},{5,4},{6,7},{7,6},{8,9},{9,8},{10,11... | collective-permute-start | bytes 11010056 | tf_op jit(solution)/shard_map/ppermute | solution.py:57
  97.0 18.5 %collective-permute-start.24 = (bf16[256,7168]{1,0:T(8,128)(2,1)}, bf16[256,7168]{1,0:T(8,128)(2,1)}, u32[]{:S(2)}, u32[]{:S(2)}) collective-permute-start(bf16[256,7168]{1,0:T(8,128)(2,1)} %bitcast.25), channel_id=1, source_target_pairs={{0,1},{1,0},{2,3},{3,2},{4,5},{5,4},{6,7},{7,6},{8,9},{9,8},{10,11... | collective-permute-start | bytes 11010056 | tf_op jit(solution)/shard_map/ppermute | solution.py:57
  124.9 35.4 %all-to-all-start = ((bf16[32,5,8,896]{3,2,1,0:T(8,128)(2,1)}), bf16[32,5,8,896]{3,2,1,0:T(8,128)(2,1)}, u32[]{:S(2)}, u32[]{:S(2)}) async-start(bf16[32,5,8,896]{3,2,1,0:T(8,128)(2,1)} %shard_map.102), calls=%async_computation | async-start | bytes 4587520 | tf_op jit(solution)/shard_map/all_to_all | solution.py:377
  132.1 2.0 copy-start
  134.2 2.0 copy-start.2
  136.2 2.0 copy-start.4
  138.3 2.0 copy-start.7
  140.3 2.0 copy-start.10
  160.3 36.1 %all-to-all-start.3 = ((bf16[32,5,8,896]{3,2,1,0:T(8,128)(2,1)}), bf16[32,5,8,896]{3,2,1,0:T(8,128)(2,1)S(1)}, u32[]{:S(2)}, u32[]{:S(2)}) async-start(bf16[32,5,8,896]{3,2,1,0:T(8,128)(2,1)} %shard_map.105), calls=%async_computation.3 | async-start | bytes 4587520 | tf_op jit(solution)/shard_map/all_to_all | solution.py:379
  167.8 2.0 copy-start.1
  169.8 2.0 copy-start.3
  171.9 2.0 copy-start.5
  189.8 13.9 %copy-start.17 = (f32[128,2]{0,1:T(2,128)S(1)}, f32[128,2]{0,1:T(2,128)}, u32[]{:S(2)}) copy-start(f32[128,2]{0,1:T(2,128)} %param.18) | copy-start | bytes 3076
  196.4 36.0 %all-to-all-start.1 = ((bf16[32,5,8,896]{3,2,1,0:T(8,128)(2,1)}), bf16[32,5,8,896]{3,2,1,0:T(8,128)(2,1)}, u32[]{:S(2)}, u32[]{:S(2)}) async-start(bf16[32,5,8,896]{3,2,1,0:T(8,128)(2,1)} %shard_map.103), calls=%async_computation.1 | async-start | bytes 4587520 | tf_op jit(solution)/shard_map/all_to_all | solution.py:379
  208.0 32.3 %collective-permute-start.26 = (bf16[4,128,896]{2,1,0:T(8,128)(2,1)}, bf16[4,128,896]{2,1,0:T(8,128)(2,1)}, u32[]{:S(2)}, u32[]{:S(2)}) collective-permute-start(bf16[4,128,896]{2,1,0:T(8,128)(2,1)} %get-tuple-element.60), channel_id=1, source_target_pairs={{0,1},{1,0},{2,3},{3,2},{4,5},{5,4},{6,7},{7,6},{8,9},{9,8},{10,11... | collective-permute-start | bytes 2752520 | tf_op jit(solution)/shard_map/ppermute | solution.py:57
  236.7 5.8 %collective-permute-start.25 = (bf16[4,128,896]{2,1,0:T(8,128)(2,1)S(1)}, bf16[4,128,896]{2,1,0:T(8,128)(2,1)}, u32[]{:S(2)}, u32[]{:S(2)}) collective-permute-start(bf16[4,128,896]{2,1,0:T(8,128)(2,1)S(1)} %get-tuple-element.57), channel_id=1, source_target_pairs={{0,1},{1,0},{2,3},{3,2},{4,5},{5,4},{6,7},{7,6},{8,9},{9,8},{10,11... | collective-permute-start | bytes 2752520 | tf_op jit(solution)/shard_map/ppermute | solution.py:57
  242.5 28.4 %copy-start.14 = (f32[128,896]{1,0:T(8,128)S(1)}, f32[128,896]{1,0:T(8,128)}, u32[]{:S(2)}) copy-start(f32[128,896]{1,0:T(8,128)} %get-tuple-element.44) | copy-start | bytes 1376260
  244.2 11.6 %collective-permute-start.27 = (bf16[128,896]{1,0:T(8,128)(2,1)S(1)}, bf16[128,896]{1,0:T(8,128)(2,1)S(1)}, u32[]{:S(2)}, u32[]{:S(2)}) collective-permute-start(bf16[128,896]{1,0:T(8,128)(2,1)S(1)} %get-tuple-element.65), channel_id=1, source_target_pairs={{0,2},{2,4},{4,6},{6,0},{1,3},{3,5},{5,7},{7,1},{8,10},{10,12},{12... | collective-permute-start | bytes 688136 | tf_op jit(solution)/shard_map/ppermute | solution.py:53
  245.4 18.4 %collective-permute-start.28 = (bf16[128,896]{1,0:T(8,128)(2,1)S(1)}, bf16[128,896]{1,0:T(8,128)(2,1)S(1)}, u32[]{:S(2)}, u32[]{:S(2)}) collective-permute-start(bf16[128,896]{1,0:T(8,128)(2,1)S(1)} %get-tuple-element.67), channel_id=1, source_target_pairs={{0,4},{2,6},{4,0},{6,2},{1,5},{3,7},{5,1},{7,3},{8,12},{10,14},{12... | collective-permute-start | bytes 688136 | tf_op jit(solution)/shard_map/ppermute | solution.py:53
  247.8 23.1 %collective-permute-start.29 = (bf16[128,896]{1,0:T(8,128)(2,1)S(1)}, bf16[128,896]{1,0:T(8,128)(2,1)S(1)}, u32[]{:S(2)}, u32[]{:S(2)}) collective-permute-start(bf16[128,896]{1,0:T(8,128)(2,1)S(1)} %get-tuple-element.66), channel_id=1, source_target_pairs={{0,6},{2,0},{4,2},{6,4},{1,7},{3,1},{5,3},{7,5},{8,14},{10,8},{12,... | collective-permute-start | bytes 688136 | tf_op jit(solution)/shard_map/ppermute | solution.py:53
  (6 other events, 10.5 us)
